TPU v7x, 128 devices: a whole 4x4x4 slice. The times are simulated.
128 devices in a mesh: ffn: 32 (over y_hi, x, z), mp: 4 (over y_lo, core).
Axes of the slice: x: 4, y: 4 (y_hi: 2, y_lo: 2; y = y_hi * 2 + y_lo), z: 4, core: 2. Of those that a mesh axis runs over, the one named last changes fastest.
Arguments:
- inputs: bfloat16 [512, 8192], P('ffn', 'mp'), may hold values from -6 to 6
- targets: bfloat16 [512, 8192], P('ffn', 'mp'), may hold values from -3 to 3
- gate_weight: bfloat16 [8192, 16384], P('mp', 'ffn'), may hold values from -0.0625 to 0.0625
- up_weight: bfloat16 [8192, 16384], P('mp', 'ffn'), may hold values from -0.0625 to 0.0625
- down_weight: bfloat16 [16384, 8192], P('ffn', 'mp'), may hold values from -0.046875 to 0.046875
- stored_vectors: bfloat16 [7, 8192, 16384], P(None, 'mp', 'ffn'), may hold values from -12 to 12, as said below
Outputs:
- next_vector: float32 [8192, 16384], P('mp', 'ffn')
- remainder_share: float32 [1], replicated
Inputs may be any that keep to these rules, and one draw needn't show every extreme that they name: `stored_vectors`: the last of the 7 vectors is the current Lanczos vector.
All inputs are finite; a program needn't handle non-finite values.
Results may differ from a plain program's by a relative error of at most 0.0049.
Values may be sent and summed in bfloat16 or wider, within the bound.
A program may use at most 128 MiB of HBM per device.

v0:
```python
import jax
import jax.numpy as jnp
from jax import lax
from jax.sharding import PartitionSpec as P

D = 8192
FF = 16384


def solve_small(gram, target_side):
    lower = jnp.linalg.cholesky(gram)
    size_count = target_side.shape[0]
    forward = []
    for row_index in range(size_count):
        running = target_side[row_index]
        for column_index in range(row_index):
            running = running - lower[row_index, column_index] * forward[column_index]
        forward.append(running / lower[row_index, row_index])
    backward = [None] * size_count
    for row_index in reversed(range(size_count)):
        running = forward[row_index]
        for column_index in range(row_index + 1, size_count):
            running = running - lower[column_index, row_index] * backward[column_index]
        backward[row_index] = running / lower[row_index, row_index]
    return jnp.stack(backward)


def against_rows(left, right):
    return lax.dot_general(
        left, right, (((1,), (1,)), ((), ())), preferred_element_type=jnp.float32
    )


def body(inputs, targets, gate_weight, up_weight, down_weight, stored_vectors):
    count = D * FF
    stored_count = stored_vectors.shape[0]
    current = stored_vectors[stored_count - 1]
    flattened = stored_vectors.reshape(stored_count, -1)
    whole_inputs = lax.all_gather(inputs, "ffn", axis=0, tiled=True)
    gate, up_values, tangent_gate = lax.psum(
        (
            jnp.dot(whole_inputs, gate_weight, preferred_element_type=jnp.float32),
            jnp.dot(whole_inputs, up_weight, preferred_element_type=jnp.float32),
            jnp.dot(whole_inputs, current, preferred_element_type=jnp.float32),
        ),
        "mp",
    )
    sigmoid_gate = jax.nn.sigmoid(gate)
    swish = gate * sigmoid_gate
    slope = sigmoid_gate * (1.0 + gate * (1.0 - sigmoid_gate))
    curve = sigmoid_gate * (1.0 - sigmoid_gate) * (2.0 + gate * (1.0 - 2.0 * sigmoid_gate))
    hidden = (swish * up_values).astype(jnp.bfloat16)
    tangent_hidden = (slope * up_values * tangent_gate).astype(jnp.bfloat16)
    own_outputs = lax.psum_scatter(
        jnp.stack(
            [
                jnp.dot(hidden, down_weight, preferred_element_type=jnp.float32),
                jnp.dot(tangent_hidden, down_weight, preferred_element_type=jnp.float32),
            ],
            axis=1,
        ),
        "ffn",
        scatter_dimension=0,
        tiled=True,
    )
    residual_pair = jnp.stack(
        [own_outputs[:, 0] - targets.astype(jnp.float32), own_outputs[:, 1]], axis=1
    ).astype(jnp.bfloat16)
    piece = lax.all_gather(residual_pair, "ffn", axis=0, tiled=True)
    adjoint_terms = jnp.stack(
        [against_rows(piece[:, 0], down_weight), against_rows(piece[:, 1], down_weight)], axis=1
    )
    adjoint_total = lax.psum(adjoint_terms, "mp")
    grad_hidden = adjoint_total[:, 0]
    tangent_grad = adjoint_total[:, 1]
    adjoint = (
        tangent_grad * up_values * slope + grad_hidden * up_values * curve * tangent_gate
    ).astype(jnp.bfloat16)
    image = lax.dot_general(
        whole_inputs, adjoint, (((0,), (0,)), ((), ())), preferred_element_type=jnp.float32
    )
    local_correlations = jnp.stack(
        [
            jnp.sum(stored_vectors[stored_index].astype(jnp.float32) * image)
            for stored_index in range(stored_count)
        ]
    )
    local_power = jnp.sum(image * image)
    correlations, gram, power = lax.psum(
        (local_correlations, against_rows(flattened, flattened), local_power), ("ffn", "mp")
    )
    gram = gram / count
    correlations = correlations / count
    power = power / count
    loadings = solve_small(gram, correlations)
    remainder = image
    for stored_index in range(stored_count):
        remainder = remainder - loadings[stored_index] * stored_vectors[stored_index].astype(
            jnp.float32
        )
    rest = lax.psum(jnp.sum(remainder * remainder), ("ffn", "mp")) / count
    next_vector = remainder / jnp.sqrt(rest + 1e-06)
    remainder_share = jnp.sqrt((rest + 1e-06) / (power + 1e-06)).reshape(1)
    return (next_vector, remainder_share)


def solution(mesh):
    return jax.shard_map(
        body,
        mesh=mesh,
        in_specs=(
            P("ffn", "mp"),
            P("ffn", "mp"),
            P("mp", "ffn"),
            P("mp", "ffn"),
            P("ffn", "mp"),
            P(None, "mp", "ffn"),
        ),
        out_specs=(P("mp", "ffn"), P()),
        check_vma=False,
    )
```

profile of v0, /device:TPU:0, one launch (start us, length us, event | category | flops | bytes accessed | tf_op | source)
XLA Modules:
  0.0 760.2 jit_solution(4319083672558102488)
XLA Ops:
  7.2 0.0 copy-start
  7.2 0.0 all-gather.3.cloned.1.call-start
  7.2 0.7 all-gather.3.cloned.1.call-update
  7.9 0.0 all-reduce.8.cloned.1.call-start
  8.0 76.6 %all-gather.3.cloned.1.call-done = bf16[512,2048]{1,0:T(8,128)(2,1)} async-done(((bf16[16,2048]{1,0:T(8,128)(2,1)}), bf16[512,2048]{1,0:T(8,128)(2,1)}) %all-gather.3.cloned.1.call-update) | async-done | bytes 2097168 | tf_op jit(solution)/shard_map/all_gather | solution.py:39
  84.5 0.0 copy-start.5
  84.5 0.0 copy-start.7
  84.5 4.6 fusion.19
  89.1 0.0 copy-done.5
  89.1 0.0 copy-done.7
  89.1 2.2 fusion.57
  91.4 0.0 copy-done.6
  91.4 2.2 fusion.58
  93.6 0.0 all-reduce.8.cloned.1.call-update
  93.7 0.0 reduce-scatter.2.cloned.1.call-start
  93.7 71.7 %all-reduce.8.cloned.1.call-done = (f32[512,512]{1,0:T(8,128)}, f32[512,512]{1,0:T(8,128)}, f32[512,512]{1,0:T(8,128)}) async-done(((f32[512,512]{1,0:T(8,128)}, f32[512,512]{1,0:T(8,128)}, f32[512,512]{1,0:T(8,128)}), (f32[512,512]{1,0:T(8,128)}, f32[512,512]{1,0:T(8,128)}, f32[512,512]{1,0:T(8,128)})) %all-reduce.8.cloned.1.call-update) | async-done | bytes 3145744 | tf_op jit(solution)/shard_map/psum | solution.py:40
  165.4 0.0 copy-done
  165.4 3.0 convolution_bitcast_fusion.1
  168.4 0.0 copy-done.8
  168.4 0.0 copy-done.9
  168.4 0.0 copy-done.10
  168.4 1.5 convolution_bitcast_fusion
  169.9 3.8 pad_maximum_fusion
  173.7 0.0 reduce-scatter.2.cloned.1.call-update
  173.8 0.0 all-gather.5.cloned.1.call-start
  173.8 204.4 %reduce-scatter.2.cloned.1.call-done = f32[16,2,2048]{2,0,1:T(8,128)} async-done(((f32[512,2,2048]{2,0,1:T(8,128)}), f32[16,2,2048]{2,0,1:T(8,128)}) %reduce-scatter.2.cloned.1.call-update) | async-done | bytes 262160 | tf_op jit(solution)/shard_map/reduce_scatter | solution.py:54
  378.2 0.9 slice.275
  379.1 0.0 copy-done.3
  379.1 0.9 fusion.45
  380.0 0.7 pad_maximum_fusion.2
  380.7 0.0 all-gather.5.cloned.1.call-update
  380.7 0.0 all-reduce.6.cloned.1.call-start
  380.8 76.2 %all-gather.5.cloned.1.call-done = bf16[512,2,2048]{2,0,1:T(8,128)(2,1)} async-done(((bf16[16,2,2048]{2,0,1:T(8,128)(2,1)}), bf16[512,2,2048]{2,0,1:T(8,128)(2,1)}) %all-gather.5.cloned.1.call-update) | async-done | bytes 4194320 | tf_op jit(solution)/shard_map/all_gather | solution.py:69
  456.9 3.0 fusion.21
  459.9 0.0 copy-done.4
  459.9 1.3 fusion.22
  461.2 1.5 pad_maximum_fusion.1
  462.8 0.0 all-reduce.6.cloned.1.call-update
  462.8 10.3 %fusion.53 = (bf16[1,2048,512]{2,1,0:T(8,128)(2,1)}, bf16[1,2048,512]{2,1,0:T(8,128)(2,1)}, bf16[1,2048,512]{2,1,0:T(8,128)(2,1)}, bf16[1,2048,512]{2,1,0:T(8,12...) fusion(bf16[7,2048,512]{2,1,0:T(8,128)(2,1)} %param.11), kind=kLoop, calls=%fused_computation.88 | loop fusion | bytes 29360128 | tf_op jit(solution)/shard_map/slice | solution.py:84
  473.1 4.0 copy.22
  477.1 4.0 copy.23
  481.1 4.0 copy.24
  485.1 4.0 copy.25
  489.0 4.0 copy.26
  493.0 4.0 copy.27
  497.0 2.4 copy.28
  499.4 44.7 %fusion.23 = f32[7,7]{0,1:T(8,128)S(1)} fusion(bf16[7,2048,512]{2,1,0:T(8,128)(2,1)} %param.11), kind=kOutput, calls=%fused_computation.48 | convolution fusion | flops 102760448 | bytes 14680260 | tf_op jit(solution)/shard_map/dot_general | solution.py:29
  544.1 0.0 all-reduce.6.cloned.1.call-done
  544.2 0.0 copy-done.2
  544.2 12.1 %fusion.16 = (f32[]{:T(128)}, f32[]{:T(128)}, f32[]{:T(128)}, f32[]{:T(128)}, f32[]{:T(128)}, /*index=5*/f32[]{:T(128)}, f32[]{:T(128)}, f32[]{:T(128)}, f32[512,2048]{1,0:T(8,128)}) fusion(bf16[1,2048,512]{1,2,0:T(8,128)(2,1)} %copy.24, bf16[1,2048,512]{1,2,0:T(8,128)(2,1)} %copy.25, bf16[1,2048,512]{1,2,0:T(8,128)(2,1)} %copy.26, ...), kind=kOutput, calls=%fused_computation.32 | convolution fusion | flops 1103101952 | bytes 26214432 | tf_op jit(solution)/shard_map/dot_general | solution.py:79
  556.3 4.5 stack.65
  560.7 64.4 %all-reduce.1 = (f32[7]{0:T(128)S(1)}, f32[7,7]{0,1:T(8,128)S(1)}) all-reduce(f32[7]{0:T(128)S(1)} %stack.65, f32[7,7]{0,1:T(8,128)S(1)} %fusion.23), channel_id=1, replica_groups=mesh['ffn'=32,'mp'=4] {'ffn','mp'}, use_global_device_ids=true, to_apply=%region_12.0 | all-reduce | flops 56 | bytes 448 | tf_op jit(solution)/shard_map/psum | solution.py:89
  625.1 0.1 copy.18
  625.2 0.6 cholesky.18
  625.9 0.7 compare_reduce_fusion
  626.6 0.6 select_select_fusion
  627.2 0.7 fusion.55
  627.9 0.7 fusion.54
  628.6 0.7 fusion.56
  668.9 9.5 %multiply_reduce_fusion = (f32[]{:T(128)}, f32[2048,512]{0,1:T(8,128)}) fusion(bf16[1,2048,512]{1,2,0:T(8,128)(2,1)S(1)} %copy-done.2, f32[]{:T(128)S(6)} %div.87, bf16[1,2048,512]{1,2,0:T(8,128)(2,1)} %copy.28, f32[]{:T(128)S(6)} %div.88, bf16[1,2048,512]{1,2,0:T(8,128)(2,1)} %copy.27, f32[]{:T(128)S(6)} %div.89, bf16[1,2048,512]{1,2,0:T(8,128)(2,1)} %copy.26, ...), kind=kLoop, calls=%fused_computation.33 | loop fusion | flops 24117248 | bytes 23068704 | tf_op jit(solution)/shard_map/reduce_sum | solution.py:101
  678.4 62.5 %all-reduce = (f32[]{:T(128)}, f32[]{:T(128)}) all-reduce(f32[]{:T(128)} %get-tuple-element.19, f32[]{:T(128)} %get-tuple-element.4), channel_id=1, replica_groups=mesh['ffn'=32,'mp'=4] {'ffn','mp'}, use_global_device_ids=true, to_apply=%region_17.18 | all-reduce | flops 2 | bytes 16 | tf_op jit(solution)/shard_map/psum | solution.py:101
  742.4 4.7 broadcast_divide_fusion
  747.0 5.5 copy.19
  752.5 0.0 copy-done.1
  (12 shorter events, 0.1 us)
Async XLA Ops:
  7.2 158.2 %copy-start = (bf16[512,2048]{1,0:T(8,128)(2,1)S(1)}, bf16[512,2048]{1,0:T(8,128)(2,1)}, u32[]{:S(2)}) copy-start(bf16[512,2048]{1,0:T(8,128)(2,1)} %param.10) | copy-start | bytes 6291460
  7.2 77.4 %all-gather.3.cloned.1.call-start = ((), (), s32[]{:S(2)}) async-start(), calls=%async_computation.1 | async-start | bytes 2162688 | tf_op jit(solution)/shard_map/all_gather | solution.py:39
  7.9 157.5 %all-reduce.8.cloned.1.call-start = ((), (), s32[]{:S(2)}) async-start(), calls=%async_computation.5 | async-start | bytes 6291456 | tf_op jit(solution)/shard_map/psum | solution.py:40
  84.5 4.6 copy-start.5
  84.5 4.6 copy-start.7
  89.1 2.3 copy-start.6
  93.7 284.5 %reduce-scatter.2.cloned.1.call-start = ((), (), s32[]{:S(2)}) async-start(), calls=%async_computation.2 | async-start | bytes 8650752 | tf_op jit(solution)/shard_map/reduce_scatter | solution.py:54
  165.4 3.0 copy-start.8
  165.4 3.0 copy-start.9
  165.4 3.0 copy-start.10
  173.7 205.3 %copy-start.3 = (bf16[16,2048]{1,0:T(8,128)(2,1)S(1)}, bf16[16,2048]{1,0:T(8,128)(2,1)}, u32[]{:S(2)}) copy-start(bf16[16,2048]{1,0:T(8,128)(2,1)} %param.7) | copy-start | bytes 196612
  173.8 283.1 %all-gather.5.cloned.1.call-start = ((), (), s32[]{:S(2)}) async-start(), calls=%async_computation.3 | async-start | bytes 4325376 | tf_op jit(solution)/shard_map/all_gather | solution.py:69
  380.7 163.4 %all-reduce.6.cloned.1.call-start = ((), (), s32[]{:S(2)}) async-start(), calls=%async_computation.4 | async-start | bytes 4194304 | tf_op jit(solution)/shard_map/psum | solution.py:73
  456.9 3.0 copy-start.4
  499.4 44.8 %copy-start.2 = (bf16[1,2048,512]{1,2,0:T(8,128)(2,1)S(1)}, bf16[1,2048,512]{1,2,0:T(8,128)(2,1)}, u32[]{:S(2)}) copy-start(bf16[1,2048,512]{1,2,0:T(8,128)(2,1)} %copy.22) | copy-start | bytes 6291460
  747.0 5.5 copy-start.1
Sparse Core Ops, SparseCore 0:
  11.1 73.3 all-gather.2
  93.8 71.5 all-reduce.7
  173.9 204.2 reduce-scatter.1
  381.6 75.2 all-gather.4
  462.9 55.0 all-reduce.5
where the time goes:
time: 762 us; the launch traced here: 760 us
  waiting for transfers between devices  430 us (56%)
  blocking collectives  127 us (17%)
  matrix products  74.7 us (10%)
  between operations  56.2 us (7%)
  local copies, waits for them, and re-layouts  49.7 us (7%)
  other arithmetic  23 us (3%)
    reduce_scatter x1, waiting for transfers between devices, body(): lax.psum_scatter(jnp.stack([jnp.dot(hidden, down_weight, preferred_elemen...  204 us
    all_gather x1, waiting for transfers between devices, body(): whole_inputs = lax.all_gather(inputs, 'ffn', axis=0, tiled=True)  76.6 us
    all_gather x1, waiting for transfers between devices, body(): piece = lax.all_gather(residual_pair, 'ffn', axis=0, tiled=True)  76.2 us
    psum x1, waiting for transfers between devices, body(): lax.psum((jnp.dot(whole_inputs, gate_weight, preferred_element_type=jnp.f...  71.7 us
    psum x1, blocking collectives, body(): lax.psum((local_correlations, against_rows(flattened, flattened), local_p...  64.4 us
    psum x1, blocking collectives, body(): rest = lax.psum(jnp.sum(remainder * remainder), ('ffn', 'mp')) / count  62.5 us
    dot_general x3, matrix products, against_rows(): lax.dot_general(left, right, (((1,), (1,)), ((), ())), preferred_element_...  49 us
    unnamed x30, local copies, waits for them, and re-layouts  31.8 us
  transfers between devices with their start and end apart: 5, of which 4 were waited for; matrix products, arithmetic and copies ran while one was open for 11% of the time, Pallas kernels for 0%

commit v1 on v0

v1 whole, which is shorter than its diff:
```python
import functools

import jax
import jax.numpy as jnp
from jax import lax
from jax.experimental import pallas as pl
from jax.experimental.pallas import tpu as pltpu
from jax.sharding import PartitionSpec as P

D = 8192
FF = 16384
STORED = 7
MESH = pl.DeviceIdType.MESH
F32 = jnp.float32
BF16 = jnp.bfloat16
PAIRS = [(j, k) for j in range(STORED) for k in range(j, STORED)]
N_GRAM = len(PAIRS)
STAT_ROWS = 40

B_Y = F32
C1 = BF16
C2 = BF16
C3 = F32


def dot(left, right):
    return jnp.dot(left, right, preferred_element_type=F32)


def dot_nt(left, right):
    return lax.dot_general(left, right, (((1,), (1,)), ((), ())), preferred_element_type=F32)


def fold(values):
    rows = values.shape[0]
    part = jnp.sum(values.reshape(rows // 8, 8, 512), axis=0)
    part = part[:, 0:128] + part[:, 128:256] + part[:, 256:384] + part[:, 384:512]
    return jnp.sum(part, axis=0, keepdims=True)


def comm_kernel(
    x_hbm, tgt_hbm, gate_hbm, up_hbm, down_hbm, stored_hbm,
    adj_out, x_out, coef_out,
    xg, tgt, gate_w, up_w, down_w, st,
    part, rb, sby, rby, tmat, gx,
    hp, a_q, b_q,
    s1, r1, s2, r2, s3, r3, rp,
    gacc, rg, sy, ry, adj,
    stat, stat_r, stat_x, stat_z,
    lsem, ssem, rsem,
):
    f = lax.axis_index("ffn")
    m = lax.axis_index("mp")
    yh, x, z = f // 16, (f // 4) % 4, f % 4
    yl, c = m // 2, m % 2
    q = c * 2 + yl
    qy = c * 2 + (1 - yl)

    def at(yh_=yh, x_=x, z_=z, yl_=yl, c_=c):
        return (yh_ * 16 + x_ * 4 + z_, yl_ * 2 + c_)

    p_core, p_yl, p_yh = at(c_=1 - c), at(yl_=1 - yl), at(yh_=1 - yh)
    xs = [(x + d) % 4 for d in (1, 2, 3)]
    zs = [(z + d) % 4 for d in (1, 2, 3)]
    p_x = [at(x_=v) for v in xs]
    p_z = [at(z_=v) for v in zs]
    peers = [p_core, p_yl, p_yh] + p_x + p_z

    counter = [0]

    def remote(src, dst, who):
        i = counter[0]
        counter[0] += 1
        return pltpu.make_async_remote_copy(
            src_ref=src, dst_ref=dst, send_sem=ssem.at[i], recv_sem=rsem.at[i],
            device_id=who, device_id_type=MESH,
        )

    def go(*copies):
        for copy in copies:
            copy.start()
        return list(copies)

    sent = []

    def go_sent(*copies):
        sent.extend(go(*copies))
        return list(copies)

    loads = [
        pltpu.make_async_copy(x_hbm.at[:, pl.ds(h * 1024, 1024)], xg.at[h, yh, x, z], lsem.at[h])
        for h in range(2)
    ]
    late = [
        pltpu.make_async_copy(stored_hbm, st, lsem.at[2]),
        pltpu.make_async_copy(gate_hbm, gate_w, lsem.at[3]),
        pltpu.make_async_copy(up_hbm, up_w, lsem.at[4]),
        pltpu.make_async_copy(down_hbm, down_w, lsem.at[5]),
        pltpu.make_async_copy(tgt_hbm, tgt, lsem.at[6]),
    ]
    go(*loads)
    go(*late)

    barrier = pltpu.get_barrier_semaphore()
    for who in peers:
        pl.semaphore_signal(barrier, inc=1, device_id=who, device_id_type=MESH)
    pl.semaphore_wait(barrier, len(peers))
    for copy in loads:
        copy.wait()

    def block(ref, h, yh_):
        return ref.at[h, yh_, x, z]

    a1 = go_sent(remote(xg.at[:, yh, x, z], xg.at[:, yh, x, z], p_yh))
    a2 = []
    for d in range(3):
        a2 += go_sent(
            remote(block(xg, 0, yh), block(xg, 0, yh), p_z[d]),
            remote(block(xg, 1, yh), block(xg, 1, yh), p_x[d]),
        )
    a1[0].wait_recv()
    for d in range(3):
        a2 += go_sent(
            remote(block(xg, 0, 1 - yh), block(xg, 0, 1 - yh), p_z[d]),
            remote(block(xg, 1, 1 - yh), block(xg, 1, 1 - yh), p_x[d]),
        )

    late[0].wait()

    def gram_range(first, last, accs):
        def step(i, accs):
            row = pl.multiple_of(i * 16, 16)
            accs = list(accs)
            for col in range(4):
                v = [
                    st[k, pl.ds(row, 16), col * 128:(col + 1) * 128].astype(F32)
                    for k in range(STORED)
                ]
                for n, (j, k) in enumerate(PAIRS):
                    prod = v[j] * v[k]
                    accs[n] = accs[n] + prod[0:8] + prod[8:16]
            return tuple(accs)

        return lax.fori_loop(first, last, step, accs)

    accs = tuple(jnp.zeros((8, 128), F32) for _ in PAIRS)
    accs = gram_range(0, 32, accs)
    for copy in a2:
        copy.wait_recv()
    a3 = []
    for d in range(3):
        a3 += go_sent(
            remote(xg.at[0, :, x], xg.at[0, :, x], p_x[d]),
            remote(xg.at[1, :, :, z], xg.at[1, :, :, z], p_z[d]),
        )
    accs = gram_range(32, 128, accs)
    for n in range(N_GRAM):
        stat[n:n + 1, :] = jnp.sum(accs[n], axis=0, keepdims=True)
    for copy in late[1:]:
        copy.wait()
    for copy in a3:
        copy.wait_recv()

    def x_rows(h, half):
        return xg[h, half].reshape(256, 1024)

    def partial(half):
        def step(n, carry):
            col = pl.multiple_of(n * 256, 256)
            cols = pl.ds(col, 256)
            left0, left1 = x_rows(0, half), x_rows(1, half)
            part[0, half, :, cols] = dot(left0, gate_w[0:1024, cols]) + dot(left1, gate_w[1024:2048, cols])
            part[1, half, :, cols] = dot(left0, up_w[0:1024, cols]) + dot(left1, up_w[1024:2048, cols])
            part[2, half, :, cols] = dot(left0, st[6, 0:1024, cols]) + dot(left1, st[6, 1024:2048, cols])
            return carry

        lax.fori_loop(0, 2, step, 0)

    partial(1 - c)
    b1 = go_sent(remote(part.at[:, 1 - c], rb, p_core))
    partial(c)
    b1[0].wait_recv()
    own = pl.ds(pl.multiple_of(yl * 128, 128), 128)
    other = pl.ds(pl.multiple_of((1 - yl) * 128, 128), 128)
    for n in range(3):
        sby[n] = (part[n, c, other, :] + rb[n, other, :]).astype(B_Y)
    b2 = go_sent(remote(sby, rby, p_yl))
    for n in range(3):
        rb[n, own, :] = rb[n, own, :] + part[n, c, own, :]
    b2[0].wait_recv()
    gate = rb[0, own, :] + rby[0].astype(F32)
    upv = rb[1, own, :] + rby[1].astype(F32)
    tang = rb[2, own, :] + rby[2].astype(F32)
    sg = 1.0 / (1.0 + jnp.exp(-gate))
    swish = gate * sg
    slope = sg * (1.0 + gate * (1.0 - sg))
    curve = sg * (1.0 - sg) * (2.0 + gate * (1.0 - 2.0 * sg))
    hp[0, q] = (swish * upv).astype(BF16)
    hp[1, q] = (slope * upv * tang).astype(BF16)
    a_q[...] = upv * slope
    b_q[...] = upv * curve * tang
    b3 = go_sent(
        remote(hp.at[:, q], hp.at[:, q], p_yl),
        remote(hp.at[:, q], hp.at[:, q], p_core),
    )
    b3[0].wait_recv()
    b4 = go_sent(remote(hp.at[:, qy], hp.at[:, qy], p_core))
    b3[1].wait_recv()
    b4[0].wait_recv()

    c1 = []
    for h in range(2):
        def out_step(i, carry, h=h):
            r = i // 4
            col = pl.multiple_of((i % 4) * 256, 256)
            left = hp[r // 2, pl.ds((r % 2) * 2, 2)].reshape(256, 512)
            right = down_w[:, pl.ds(pl.multiple_of(h * 1024 + col, 256), 256)]
            s1[h, r, :, :, :, pl.ds(col, 256)] = dot(left, right).astype(C1).reshape(4, 4, 16, 256)
            return carry

        lax.fori_loop(0, 16, out_step, 0)
        for d in range(3):
            if h == 0:
                c1 += go_sent(remote(s1.at[0, :, :, zs[d]], r1.at[0, d], p_z[d]))
            else:
                c1 += go_sent(remote(s1.at[1, :, xs[d]], r1.at[1, d], p_x[d]))

    def tm_step(i, carry):
        k = i // 4
        half = (i // 2) % 2
        cols = pl.ds(pl.multiple_of((i % 2) * 256, 256), 256)
        tmat[k, pl.ds(pl.multiple_of(half * 256, 256), 256), cols] = (
            dot(x_rows(0, half), st[k, 0:1024, cols]) + dot(x_rows(1, half), st[k, 1024:2048, cols])
        )
        return carry

    lax.fori_loop(0, 24, tm_step, 0)

    def gx_step(i, carry):
        r, s = i // 2, i % 2
        value = dot_nt(x_rows(0, r), x_rows(0, s)) + dot_nt(x_rows(1, r), x_rows(1, s))
        rows = pl.ds(pl.multiple_of(r * 256, 256), 256)
        cols = pl.ds(pl.multiple_of(s * 256, 256), 256)
        high = value.astype(BF16)
        gx[0, rows, cols] = high
        gx[1, rows, cols] = (value - high.astype(F32)).astype(BF16)
        return carry

    lax.fori_loop(0, 4, gx_step, 0)

    xo = pltpu.make_async_copy(xg, x_out, lsem.at[7])
    xo.start()

    c2 = []
    for h in range(2):
        for d in range(3):
            c1[h * 3 + d].wait_recv()

        def sum_step(i, carry, h=h):
            r, g = i // 4, i % 4
            mine = s1[0, r, g, z] if h == 0 else s1[1, r, x, g]
            total = mine.astype(F32)
            for d in range(3):
                total = total + r1[h, d, r, g].astype(F32)
            s2[h, r, g] = total.astype(C2)
            return carry

        lax.fori_loop(0, 16, sum_step, 0)
        for d in range(3):
            if h == 0:
                c2 += go_sent(remote(s2.at[0, :, xs[d]], r2.at[0, d], p_x[d]))
            else:
                c2 += go_sent(remote(s2.at[1, :, zs[d]], r2.at[1, d], p_z[d]))
    for copy in c2:
        copy.wait_recv()
    for h in range(2):
        for p in range(2):
            for w in range(2):
                r = p * 2 + w
                mine = s2[0, r, x] if h == 0 else s2[1, r, z]
                total = mine.astype(F32)
                for d in range(3):
                    total = total + r2[h, d, r].astype(F32)
                s3[h, p, w] = total.astype(C3)
    c3 = go_sent(remote(s3.at[:, :, 1 - yh], r3, p_yh))
    c3[0].wait_recv()
    for h in range(2):
        for p in range(2):
            total = s3[h, p, yh].astype(F32) + r3[h, p].astype(F32)
            if p == 0:
                total = total - tgt[:, h * 1024:(h + 1) * 1024].astype(F32)
            rp[h, p, yh, x, z] = total.astype(BF16)

    own_rp = rp.at[:, :, yh, x, z]
    d1 = go_sent(remote(own_rp, own_rp, p_yh))
    d1[0].wait_recv()
    d2 = []
    for d in range(3):
        for h in range(2):
            ref = rp.at[h, :, :, x, z]
            d2 += go_sent(remote(ref, ref, (p_x, p_z)[h][d]))
    for copy in d2:
        copy.wait_recv()
    d3 = []
    for d in range(3):
        ref0, ref1 = rp.at[0, :, :, :, z], rp.at[1, :, :, x]
        d3 += go_sent(remote(ref0, ref0, p_z[d]), remote(ref1, ref1, p_x[d]))
    for copy in d3:
        copy.wait_recv()

    def grad(half):
        for p in range(2):
            def step(n, carry, p=p):
                cols = pl.ds(pl.multiple_of(n * 256, 256), 256)
                value = dot_nt(rp[0, p, half].reshape(256, 1024), down_w[cols, 0:1024])
                value = value + dot_nt(rp[1, p, half].reshape(256, 1024), down_w[cols, 1024:2048])
                gacc[p, half, :, cols] = value
                return carry

            lax.fori_loop(0, 2, step, 0)

    grad(1 - c)
    e1 = go_sent(remote(gacc.at[:, 1 - c], rg, p_core))
    grad(c)
    e1[0].wait_recv()
    for p in range(2):
        sy[p] = gacc[p, c, other, :] + rg[p, other, :]
    e2 = go_sent(remote(sy, ry, p_yl))
    e2[0].wait_recv()
    gh = gacc[0, c, own, :] + rg[0, own, :] + ry[0]
    tg = gacc[1, c, own, :] + rg[1, own, :] + ry[1]
    adj[q] = (tg * a_q[...] + gh * b_q[...]).astype(BF16)
    e3 = go_sent(
        remote(adj.at[q], adj.at[q], p_yl),
        remote(adj.at[q], adj.at[q], p_core),
    )
    e3[0].wait_recv()
    e4 = go_sent(remote(adj.at[qy], adj.at[qy], p_core))
    e3[1].wait_recv()
    e4[0].wait_recv()
    ao = pltpu.make_async_copy(adj, adj_out, lsem.at[8])
    ao.start()

    for k in range(STORED):
        total = jnp.zeros((1, 128), F32)
        for i in range(4):
            left = part[2, i // 2, (i % 2) * 128:(i % 2) * 128 + 128, :] if k == 6 else tmat[k, i * 128:i * 128 + 128, :]
            total = total + fold(left * adj[i].astype(F32))
        stat[N_GRAM + k:N_GRAM + k + 1, :] = total
    whole = adj[...].reshape(512, 512)
    total = jnp.zeros((1, 128), F32)
    for i in range(2):
        rows = slice(i * 256, i * 256 + 256)
        mixed = dot(gx[0, rows, :], whole) + dot(gx[1, rows, :], whole)
        total = total + fold(mixed * whole[i * 256:i * 256 + 256].astype(F32))
    stat[N_GRAM + 7:N_GRAM + 8, :] = total
    stat[N_GRAM + 8:STAT_ROWS, :] = jnp.zeros((STAT_ROWS - N_GRAM - 8, 128), F32)

    for n, who in enumerate((p_core, p_yl, p_yh)):
        sc = go_sent(remote(stat.at[pl.ds(n * STAT_ROWS, STAT_ROWS)], stat_r.at[n], who))
        sc[0].wait_recv()
        both = stat[n * STAT_ROWS:(n + 1) * STAT_ROWS, :] + stat_r[n]
        if n < 2:
            stat[(n + 1) * STAT_ROWS:(n + 2) * STAT_ROWS, :] = both
    stat_x[x] = both
    sc = go_sent(*[remote(stat_x.at[x], stat_x.at[x], p_x[d]) for d in range(3)])
    for copy in sc:
        copy.wait_recv()
    stat_z[z] = (stat_x[0] + stat_x[1]) + (stat_x[2] + stat_x[3])
    sc = go_sent(*[remote(stat_z.at[z], stat_z.at[z], p_z[d]) for d in range(3)])
    for copy in sc:
        copy.wait_recv()
    total = (stat_z[0] + stat_z[1]) + (stat_z[2] + stat_z[3])
    means = jnp.sum(total, axis=1, keepdims=True) * (1.0 / (D * FF))
    value = [means[n:n + 1, :] for n in range(N_GRAM + 8)]
    gram = {}
    for n, (j, k) in enumerate(PAIRS):
        gram[j, k] = gram[k, j] = value[n]
    corr = value[N_GRAM:N_GRAM + 7]
    power = value[N_GRAM + 7]
    lower = {}
    inverse = []
    for j in range(STORED):
        pivot = gram[j, j]
        for n in range(j):
            pivot = pivot - lower[j, n] * lower[j, n]
        pivot = jnp.sqrt(pivot)
        inverse.append(1.0 / pivot)
        for i in range(j + 1, STORED):
            entry = gram[i, j]
            for n in range(j):
                entry = entry - lower[i, n] * lower[j, n]
            lower[i, j] = entry * inverse[j]
    forward = []
    for j in range(STORED):
        running = corr[j]
        for n in range(j):
            running = running - lower[j, n] * forward[n]
        forward.append(running * inverse[j])
    load = [None] * STORED
    for j in reversed(range(STORED)):
        running = forward[j]
        for n in range(j + 1, STORED):
            running = running - lower[n, j] * load[n]
        load[j] = running * inverse[j]
    rest = power
    for j in range(STORED):
        inner = -2.0 * corr[j]
        for k in range(STORED):
            inner = inner + gram[j, k] * load[k]
        rest = rest + load[j] * inner
    rest = jnp.maximum(rest, 0.0)
    scale = 1.0 / jnp.sqrt(rest + 1e-06)
    share = jnp.sqrt((rest + 1e-06) / (power + 1e-06))
    rows = [-(load[j] * scale) for j in range(STORED)] + [scale, share]
    rows = rows + [jnp.zeros((1, 1), F32)] * (16 - len(rows))
    for n in range(16):
        coef_out[n:n + 1, :] = jnp.broadcast_to(rows[n], (1, 128))

    for copy in sent:
        copy.wait_send()
    xo.wait()
    ao.wait()


def final_kernel(coef, x_ref, adj_ref, st_ref, out_ref, share_ref):
    @pl.when(pl.program_id(0) == 0)
    def _():
        share_ref[0] = coef[8, 0]

    left = x_ref[0].reshape(512, x_ref.shape[-1])
    image = lax.dot_general(
        left, adj_ref[...], (((0,), (0,)), ((), ())), preferred_element_type=F32
    )
    total = image * coef[7, 0]
    for k in range(STORED):
        total = total + coef[k, 0] * st_ref[k].astype(F32)
    out_ref[...] = total


def body(inputs, targets, gate_weight, up_weight, down_weight, stored_vectors):
    any_spec = pl.BlockSpec(memory_space=pl.ANY)
    n_copies = 70
    adj, xg, coef = pl.pallas_call(
        comm_kernel,
        out_shape=(
            jax.ShapeDtypeStruct((4, 128, 512), BF16),
            jax.ShapeDtypeStruct((2, 2, 4, 4, 16, 1024), BF16),
            jax.ShapeDtypeStruct((16, 128), F32),
        ),
        in_specs=[any_spec] * 6,
        out_specs=(any_spec, any_spec, pl.BlockSpec(memory_space=pltpu.VMEM)),
        scratch_shapes=[
            pltpu.VMEM((2, 2, 4, 4, 16, 1024), BF16),
            pltpu.VMEM((16, 2048), BF16),
            pltpu.VMEM((2048, 512), BF16),
            pltpu.VMEM((2048, 512), BF16),
            pltpu.VMEM((512, 2048), BF16),
            pltpu.VMEM((STORED, 2048, 512), BF16),
            pltpu.VMEM((3, 2, 256, 512), F32),
            pltpu.VMEM((3, 256, 512), F32),
            pltpu.VMEM((3, 128, 512), B_Y),
            pltpu.VMEM((3, 128, 512), B_Y),
            pltpu.VMEM((STORED - 1, 512, 512), F32),
            pltpu.VMEM((2, 512, 512), BF16),
            pltpu.VMEM((2, 4, 128, 512), BF16),
            pltpu.VMEM((128, 512), F32),
            pltpu.VMEM((128, 512), F32),
            pltpu.VMEM((2, 4, 4, 4, 16, 1024), C1),
            pltpu.VMEM((2, 3, 4, 4, 16, 1024), C1),
            pltpu.VMEM((2, 4, 4, 16, 1024), C2),
            pltpu.VMEM((2, 3, 4, 16, 1024), C2),
            pltpu.VMEM((2, 2, 2, 16, 1024), C3),
            pltpu.VMEM((2, 2, 16, 1024), C3),
            pltpu.VMEM((2, 2, 2, 4, 4, 16, 1024), BF16),
            pltpu.VMEM((2, 2, 256, 512), F32),
            pltpu.VMEM((2, 256, 512), F32),
            pltpu.VMEM((2, 128, 512), F32),
            pltpu.VMEM((2, 128, 512), F32),
            pltpu.VMEM((4, 128, 512), BF16),
            pltpu.VMEM((3 * STAT_ROWS, 128), F32),
            pltpu.VMEM((3, STAT_ROWS, 128), F32),
            pltpu.VMEM((4, STAT_ROWS, 128), F32),
            pltpu.VMEM((4, STAT_ROWS, 128), F32),
            pltpu.SemaphoreType.DMA((9,)),
            pltpu.SemaphoreType.DMA((n_copies,)),
            pltpu.SemaphoreType.DMA((n_copies,)),
        ],
        compiler_params=pltpu.CompilerParams(
            collective_id=0, has_side_effects=True, vmem_limit_bytes=62 * 2**20
        ),
        name="exchange",
    )(inputs, targets, gate_weight, up_weight, down_weight, stored_vectors)

    tile = 128
    per_half = 1024 // tile
    next_vector, share = pl.pallas_call(
        final_kernel,
        grid=(2048 // tile,),
        out_shape=(
            jax.ShapeDtypeStruct((2048, 512), F32),
            jax.ShapeDtypeStruct((1,), F32),
        ),
        in_specs=[
            pl.BlockSpec(memory_space=pltpu.SMEM),
            pl.BlockSpec((1, 512, tile), lambda i: (i // per_half, 0, i % per_half)),
            pl.BlockSpec((512, 512), lambda i: (0, 0)),
            pl.BlockSpec((STORED, tile, 512), lambda i: (0, i, 0)),
        ],
        out_specs=(
            pl.BlockSpec((tile, 512), lambda i: (i, 0)),
            pl.BlockSpec(memory_space=pltpu.SMEM),
        ),
        compiler_params=pltpu.CompilerParams(vmem_limit_bytes=32 * 2**20),
        name="finish",
    )(coef, xg.reshape(2, 512, 1024), adj.reshape(512, 512), stored_vectors)
    return next_vector, share


def solution(mesh):
    return jax.shard_map(
        body,
        mesh=mesh,
        in_specs=(
            P("ffn", "mp"),
            P("ffn", "mp"),
            P("mp", "ffn"),
            P("mp", "ffn"),
            P("ffn", "mp"),
            P(None, "mp", "ffn"),
        ),
        out_specs=(P("mp", "ffn"), P()),
        check_vma=False,
    )
```

time: 762 us -> 208 us (0.27)
  waiting for transfers between devices: 430 us -> 0 us
  Pallas kernels: 0 us -> 199 us
  blocking collectives: 127 us -> 0 us
  matrix products: 74.7 us -> 0 us
  between operations: 56.2 us -> 0.65 us
  local copies, waits for them, and re-layouts: 49.7 us -> 8.5 us
  other arithmetic: 23 us -> 0 us
    reduce_scatter x1 -> x0, waiting for transfers between devices: 204 us -> none  [body(): lax.psum_scatter(jnp.stack([jnp.dot(hidden, down_weight, preferred_elemen...]
    pallas_call x0 -> x2, Pallas kernels: none -> 199 us  [the longest x1 188 us: body(): pl.pallas_call(comm_kernel, out_shape=(jax.ShapeDtypeStruct((4, 128, 512)...]
    all_gather x2 -> x0, waiting for transfers between devices: 153 us -> none  [the longest x1 76.6 us: body(): whole_inputs = lax.all_gather(inputs, 'ffn', axis=0, tiled=True)]
    psum x2 -> x0, blocking collectives: 127 us -> none  [the longest x1 64.4 us: body(): lax.psum((local_correlations, against_rows(flattened, flattened), local_p...]
    dot_general x9 -> x0, matrix products: 74.7 us -> none  [the longest x3 49 us: against_rows(): lax.dot_general(left, right, (((1,), (1,)), ((), ())), preferred_element_...]
    psum x2 -> x0, waiting for transfers between devices: 71.7 us -> none  [the longest x1 71.7 us: body(): lax.psum((jnp.dot(whole_inputs, gate_weight, preferred_element_type=jnp.f...]
    unnamed x30 -> x8, local copies, waits for them, and re-layouts: 31.8 us -> 8.5 us
    slice x5 -> x0, local copies, waits for them, and re-layouts: 13.3 us -> none  [the longest x1 10.3 us: body(): stored_vectors[stored_index].astype(jnp.float32) * image]
  transfers between devices with their start and end apart: 5 -> 0, of which waited for: 4 -> 0; matrix products, arithmetic and copies ran while one was open for 11% -> 0% of each run, Pallas kernels for 0% -> 0%
where the time goes in v1:
time: 208 us
  Pallas kernels  199 us (96%)
  local copies, waits for them, and re-layouts  8.5 us (4%)
    pallas_call x1, Pallas kernels, body(): pl.pallas_call(comm_kernel, out_shape=(jax.ShapeDtypeStruct((4, 128, 512)...  188 us
    pallas_call x1, Pallas kernels, body(): pl.pallas_call(final_kernel, grid=(2048 // tile,), out_shape=(jax.ShapeDt...  10.3 us
    unnamed x8, local copies, waits for them, and re-layouts  8.5 us

profile of v1, /device:TPU:0, one launch (start us, length us, event | category | flops | bytes accessed | tf_op | source)
XLA Modules:
  0.0 207.8 jit_solution(7992428208682957644)
XLA Ops:
  0.6 188.3 %exchange.1 = (bf16[4,128,512]{2,1,0:T(8,128)(2,1)}, bf16[2,2,4,4,16,1024]{5,4,3,2,1,0:T(8,128)(2,1)}, f32[16,128]{1,0:T(8,128)}) custom-call(bf16[16,2048]{1,0:T(8,128)(2,1)} %x_hbm.1, bf16[16,2048]{1,0:T(8,128)(2,1)} %tgt_hbm.1, bf16[2048,512]{1,0:T(8,128)(2,1)} %gate_hbm.1, bf16[2048,512]{1,0:T(8,128)(2,1)} %up_hbm.1, bf16[512,2048]{1,0:T(8,128)(2,1)} %down_hbm.1, ...), custom_call_target="tpu_custom_call" | custom-call | tf_op jit(solution)/shard_map/exchange/pallas_call | solution.py:444
  188.9 0.0 copy-start
  189.0 5.2 %copy-done = bf16[7,2048,512]{2,1,0:T(8,128)(2,1)S(1)} copy-done((bf16[7,2048,512]{2,1,0:T(8,128)(2,1)S(1)}, bf16[7,2048,512]{2,1,0:T(8,128)(2,1)}, u32[]{:S(2)}) %copy-start) | copy-done | bytes 14680088
  194.1 0.0 copy-start.1
  194.1 1.6 copy-done.1
  195.7 0.0 copy-start.2
  195.7 1.0 copy-done.2
  196.8 0.0 copy-start.3
  196.8 0.7 copy-done.3
  197.5 10.3 %finish.1 = (f32[2048,512]{1,0:T(8,128)}, f32[1]{0:T(128)}) custom-call(f32[16,128]{1,0:T(8,128)S(1)} %copy-done.3, bf16[2,512,1024]{2,1,0:T(8,128)(2,1)S(1)} %bitcast.2, bf16[512,512]{1,0:T(8,128)(2,1)S(1)} %bitcast.3, bf16[7,2048,512]{2,1,0:T(8,128)(2,1)S(1)} %copy-done), custom_call_target="tpu_custom_call" | custom-call | tf_op jit(solution)/shard_map/finish/pallas_call | solution.py:497
Async XLA Ops:
  188.9 5.2 %copy-start = (bf16[7,2048,512]{2,1,0:T(8,128)(2,1)S(1)}, bf16[7,2048,512]{2,1,0:T(8,128)(2,1)}, u32[]{:S(2)}) copy-start(bf16[7,2048,512]{2,1,0:T(8,128)(2,1)} %st_ref.1) | copy-start | bytes 44040196
  194.1 1.6 copy-start.1
  195.7 1.0 copy-start.2
  196.8 0.7 copy-start.3

commit v2 on v1

v2 whole, which is shorter than its diff:
```python
import functools

import jax
import jax.numpy as jnp
from jax import lax
from jax.experimental import pallas as pl
from jax.experimental.pallas import tpu as pltpu
from jax.sharding import PartitionSpec as P

D = 8192
FF = 16384
STORED = 7
MESH = pl.DeviceIdType.MESH
F32 = jnp.float32
BF16 = jnp.bfloat16
PAIRS = [(j, k) for j in range(STORED) for k in range(j, STORED)]
N_GRAM = len(PAIRS)

B_Y = BF16
C1 = BF16
C2 = BF16
C3 = BF16
E_Y = BF16
S = 4
W = 1024 // S
J = 2


def dot(left, right):
    return jnp.dot(left, right, preferred_element_type=F32)


def dot_nt(left, right):
    return lax.dot_general(left, right, (((1,), (1,)), ((), ())), preferred_element_type=F32)


def fold(values):
    rows, lanes = values.shape
    part = jnp.sum(values.reshape(rows // 8, 8, lanes), axis=0)
    total = part[:, 0:128]
    for n in range(1, lanes // 128):
        total = total + part[:, n * 128:n * 128 + 128]
    return jnp.sum(total, axis=0, keepdims=True)


def comm_kernel(
    x_hbm, tgt_hbm, gate_hbm, up_hbm, down_hbm, stored_hbm,
    adj_out, x_out, coef_out,
    xg, tgt, gate_w, up_w, down_w, st,
    part, rb, sby, rby, tmat, gx,
    hp, ab, s1, r1, s2, s2_own, r2, s3, s3_own, r3, rp,
    gacc, pa, rg, sy, ry, adj,
    stat_g, slot_gy, slot_gx, stat_c, slot_cy, slot_cx,
    lsem, ssem, rsem,
):
    f = lax.axis_index("ffn")
    m = lax.axis_index("mp")
    yh, x, z = f // 16, (f // 4) % 4, f % 4
    yl, c = m // 2, m % 2
    q = c * 2 + yl
    qy = c * 2 + (1 - yl)

    def at(yh_=yh, x_=x, z_=z, yl_=yl, c_=c):
        return (yh_ * 16 + x_ * 4 + z_, yl_ * 2 + c_)

    xs = [(x + d) % 4 for d in (1, 3, 2)]
    zs = [(z + d) % 4 for d in (1, 3, 2)]
    p_x = [at(x_=v) for v in xs]
    p_z = [at(z_=v) for v in zs]
    p_yc = [
        at(yh_=(yh + i) % 2, yl_=(yl + j) % 2, c_=(c + k) % 2)
        for i in range(2) for j in range(2) for k in range(2) if i + j + k > 0
    ]
    p_xz = [
        at(x_=(x + i) % 4, z_=(z + j) % 4) for i in range(4) for j in range(4) if i + j > 0
    ]
    p_core, p_yl, p_yh = at(c_=1 - c), at(yl_=1 - yl), at(yh_=1 - yh)
    peers = p_yc + p_xz

    counter = [0]

    def remote(src, dst, who):
        i = counter[0]
        counter[0] += 1
        return pltpu.make_async_remote_copy(
            src_ref=src, dst_ref=dst, send_sem=ssem.at[i], recv_sem=rsem.at[i],
            device_id=who, device_id_type=MESH,
        )

    sent = []

    def go(*copies):
        for copy in copies:
            copy.start()
        return list(copies)

    def go_sent(*copies):
        sent.extend(go(*copies))
        return list(copies)

    loads = [
        pltpu.make_async_copy(x_hbm.at[:, pl.ds(h * 1024, 1024)], xg.at[h, yh, x, z], lsem.at[h])
        for h in range(2)
    ]
    late = [
        pltpu.make_async_copy(gate_hbm, gate_w, lsem.at[2]),
        pltpu.make_async_copy(up_hbm, up_w, lsem.at[3]),
        pltpu.make_async_copy(stored_hbm, st, lsem.at[4]),
        pltpu.make_async_copy(down_hbm, down_w, lsem.at[5]),
        pltpu.make_async_copy(tgt_hbm, tgt, lsem.at[6]),
    ]
    go(*loads)
    go(*late)

    barrier = pltpu.get_barrier_semaphore()
    for who in peers:
        pl.semaphore_signal(barrier, inc=1, device_id=who, device_id_type=MESH)
    for j in range(J):
        for n in range(3):
            part[j, n] = jnp.zeros(part.shape[2:], F32)
    pl.semaphore_wait(barrier, len(peers))
    for copy in loads:
        copy.wait()

    def block(h, yh_):
        return xg.at[h, yh_, x, z]

    a1 = go_sent(remote(xg.at[:, yh, x, z], xg.at[:, yh, x, z], p_yh))
    a2 = {}
    a3 = {}

    def second(i, w):
        a2[i] = []
        for d in range(3):
            a2[i] += go_sent(
                remote(block(0, w), block(0, w), p_z[d]),
                remote(block(1, w), block(1, w), p_x[d]),
            )

    def third(i, w):
        for copy in a2[i]:
            copy.wait_recv()
        a3[i] = []
        for d in range(3):
            a3[i] += go_sent(
                remote(xg.at[0, w, x], xg.at[0, w, x], p_x[d]),
                remote(xg.at[1, w, :, z], xg.at[1, w, :, z], p_z[d]),
            )

    mine, far = yh, 1 - yh
    second(0, mine)
    a1[0].wait_recv()
    second(1, far)
    third(0, mine)
    third(1, far)
    for copy in late:
        copy.wait()

    def partial(h, line):
        def step(j, carry):
            cols = pl.ds(pl.multiple_of(j * 256, 256), 256)
            left = (xg[0, :, line] if h == 0 else xg[1, :, :, line]).reshape(128, 1024)
            depth = slice(h * 1024, h * 1024 + 1024)
            for n in range(3):
                right = (gate_w, up_w)[n][depth, cols] if n < 2 else st[6, depth, cols]
                value = dot(left, right).reshape(2, 4, 16, 256)
                if h == 0:
                    part[j, n, :, line] = part[j, n, :, line] + value
                else:
                    part[j, n, :, :, line] = part[j, n, :, :, line] + value
            return carry

        lax.fori_loop(0, J, step, 0)

    partial(0, x)
    partial(1, z)
    for d, source in ((0, 1), (1, 0), (2, 2)):
        a3[0][2 * d].wait_recv()
        a3[1][2 * d].wait_recv()
        partial(0, xs[source])
        a3[0][2 * d + 1].wait_recv()
        a3[1][2 * d + 1].wait_recv()
        partial(1, zs[source])

    b1 = []
    for j in range(J):
        b1 += go_sent(remote(part.at[j, :, 1 - c], rb.at[j], p_core))
    b2 = []
    for j in range(J):
        b1[j].wait_recv()
        for n in range(3):
            for i in range(2):
                g = (1 - yl) * 2 + i
                sby[j, n, i] = (part[j, n, c, g] + rb[j, n, g]).astype(B_Y)
        b2 += go_sent(remote(sby.at[j], rby.at[j], p_yl))
    b3 = []
    for j in range(J):
        cols = slice(j * 256, j * 256 + 256)
        sums = []
        b2[j].wait_recv()
        for n in range(3):
            halves = []
            for i in range(2):
                g = yl * 2 + i
                halves.append(part[j, n, c, g] + rb[j, n, g] + rby[j, n, i].astype(F32))
            sums.append(jnp.concatenate([v.reshape(64, 256) for v in halves], axis=0))
        gate, upv, tang = sums
        sg = 1.0 / (1.0 + jnp.exp(-gate))
        swish = gate * sg
        slope = sg * (1.0 + gate * (1.0 - sg))
        curve = sg * (1.0 - sg) * (2.0 + gate * (1.0 - 2.0 * sg))
        hp[j, 0, q] = (swish * upv).astype(BF16)
        hp[j, 1, q] = (slope * upv * tang).astype(BF16)
        ref = hp.at[j, :, q]
        b3.append(go_sent(remote(ref, ref, p_yl), remote(ref, ref, p_core)))
        ab[0, q, :, cols] = upv * slope
        ab[1, q, :, cols] = upv * curve * tang
    b4 = []
    for j in range(J):
        b3[j][0].wait_recv()
        ref = hp.at[j, :, qy]
        b4 += go_sent(remote(ref, ref, p_core))
    for j in range(J):
        b3[j][1].wait_recv()
        b4[j].wait_recv()

    own_ab = ab.at[:, q]
    ab1 = go_sent(remote(own_ab, own_ab, p_yl), remote(own_ab, own_ab, p_core))
    c1, c2, c3, d1, d2, d3, d4 = {}, {}, {}, {}, {}, {}, {}

    def c1_issue(s):
        c1[s] = []
        for h in range(2):
            def out_step(r, carry, h=h):
                wide = slice(h * 1024 + s * W, h * 1024 + s * W + W)
                value = jnp.zeros((256, W), F32)
                for j in range(J):
                    left = hp[j, r // 2, pl.ds((r % 2) * 2, 2)].reshape(256, 256)
                    value = value + dot(left, down_w[j * 256:j * 256 + 256, wide])
                s1[s, h, r] = value.astype(C1).reshape(4, 4, 16, W)
                return carry

            lax.fori_loop(0, 4, out_step, 0)
            for d in range(3):
                if h == 0:
                    c1[s] += go_sent(remote(s1.at[s, 0, :, :, zs[d]], r1.at[s, 0, d], p_z[d]))
                else:
                    c1[s] += go_sent(remote(s1.at[s, 1, :, xs[d]], r1.at[s, 1, d], p_x[d]))

    def c2_issue(s):
        for h in range(2):
            for d in range(3):
                c1[s][h * 3 + d].wait_recv()

            def sum_step(i, carry, h=h):
                p, g = i // 4, i % 4
                for own in range(2):
                    w = yh if own else 1 - yh
                    r = p * 2 + w
                    here = s1[s, 0, r, g, z] if h == 0 else s1[s, 1, r, x, g]
                    total = here.astype(F32)
                    for d in range(3):
                        total = total + r1[s, h, d, r, g].astype(F32)
                    if own:
                        s2_own[s, h, p, g] = total
                    else:
                        s2[s, h, p, g] = total.astype(C2)
                return carry

            lax.fori_loop(0, 8, sum_step, 0)
        c2[s] = go_sent(remote(s2.at[s], r2.at[s], p_yh))

    def c3_issue(s):
        c2[s][0].wait_recv()
        c3[s] = []
        for h in range(2):
            for p in range(2):
                total = s2_own[s, h, p] + r2[s, h, p].astype(F32)
                s3_own[s, h, p] = total
                s3[s, h, p] = total.astype(C3)
            for d in range(3):
                if h == 0:
                    c3[s] += go_sent(remote(s3.at[s, 0, :, xs[d]], r3.at[s, 0, d], p_x[d]))
                else:
                    c3[s] += go_sent(remote(s3.at[s, 1, :, zs[d]], r3.at[s, 1, d], p_z[d]))

    def d1_issue(s):
        for copy in c3[s]:
            copy.wait_recv()
        d1[s] = []
        for h in range(2):
            for p in range(2):
                total = s3_own[s, h, p, x if h == 0 else z]
                for d in range(3):
                    total = total + r3[s, h, d, p].astype(F32)
                if p == 0:
                    wide = slice(h * 1024 + s * W, h * 1024 + s * W + W)
                    total = total - tgt[:, wide].astype(F32)
                rp[s, h, p, yh, x, z] = total.astype(BF16)
            ref = rp.at[s, h, :, yh, x, z]
            for d in range(3):
                d1[s] += go_sent(remote(ref, ref, (p_x, p_z)[h][d]))

    def d2_issue(s):
        for copy in d1[s]:
            copy.wait_recv()
        ref0, ref1 = rp.at[s, 0, :, yh, :, z], rp.at[s, 1, :, yh, x]
        d2[s] = go_sent(remote(ref0, ref0, p_yh), remote(ref1, ref1, p_yh))

    def d3_issue(s):
        for copy in d2[s]:
            copy.wait_recv()
        d3[s] = []
        for d in range(2):
            ref0, ref1 = rp.at[s, 0, :, :, :, z], rp.at[s, 1, :, :, x]
            d3[s] += go_sent(remote(ref0, ref0, p_z[d]), remote(ref1, ref1, p_x[d]))

    def d4_issue(s):
        d4[s] = []
        for d in range(2):
            d3[s][2 * d].wait_recv()
            ref = rp.at[s, 0, d, :, :, zs[1 - d]]
            d4[s] += go_sent(remote(ref, ref, p_z[d]))
            d3[s][2 * d + 1].wait_recv()
            ref = rp.at[s, 1, d, :, xs[1 - d]]
            d4[s] += go_sent(remote(ref, ref, p_x[d]))

    c1_issue(0)
    c1_issue(1)

    def x_rows(h, half):
        return xg[h, half].reshape(256, 1024)

    def tm_step(i, carry):
        k = i // 4
        half = (i // 2) % 2
        cols = pl.ds(pl.multiple_of((i % 2) * 256, 256), 256)
        tmat[k, pl.ds(pl.multiple_of(half * 256, 256), 256), cols] = (
            dot(x_rows(0, half), st[k, 0:1024, cols]) + dot(x_rows(1, half), st[k, 1024:2048, cols])
        )
        return carry

    def gx_step(i, carry):
        r, t = i // 2, i % 2
        value = dot_nt(x_rows(0, r), x_rows(0, t)) + dot_nt(x_rows(1, r), x_rows(1, t))
        rows = pl.ds(pl.multiple_of(r * 256, 256), 256)
        cols = pl.ds(pl.multiple_of(t * 256, 256), 256)
        high = value.astype(BF16)
        gx[0, rows, cols] = high
        gx[1, rows, cols] = (value - high.astype(F32)).astype(BF16)
        return carry

    xo = pltpu.make_async_copy(xg, x_out, lsem.at[7])
    xo.start()

    def grad_step(s, i):
        p, half, n = i // 4, (i // 2) % 2, i % 2
        rows = pl.ds(pl.multiple_of(n * 256, 256), 256)
        value = dot_nt(rp[s, 0, p, half].reshape(256, W), down_w[rows, s * W:s * W + W])
        value = value + dot_nt(
            rp[s, 1, p, half].reshape(256, W), down_w[rows, 1024 + s * W:1024 + s * W + W]
        )
        if s > 0:
            value = value + gacc[p, half, :, rows]
        gacc[p, half, :, rows] = value

    def grad(s):
        def step(i, carry):
            grad_step(s, i)
            return carry

        lax.fori_loop(0, 8, step, 0)

    def all_sum(stat, slot_y, slot_x):
        mine = (yh * 2 + yl) * 2 + c
        slot_y[mine] = stat[...]
        ref = slot_y.at[mine]
        first = go_sent(*[remote(ref, ref, who) for who in p_yc])
        yield
        for copy in first:
            copy.wait_recv()
        total = slot_y[0]
        for i in range(1, 8):
            total = total + slot_y[i]
        here = x * 4 + z
        slot_x[here] = total
        ref = slot_x.at[here]
        second = go_sent(*[remote(ref, ref, who) for who in p_xz])
        yield
        for copy in second:
            copy.wait_recv()
        total = slot_x[0]
        for i in range(1, 16):
            total = total + slot_x[i]
        yield jnp.sum(total, axis=1, keepdims=True) * (1.0 / (D * FF))

    def gram_range(first, last, accs):
        def step(i, accs):
            row = pl.multiple_of(i * 16, 16)
            accs = list(accs)
            for col in range(4):
                v = [
                    st[k, pl.ds(row, 16), col * 128:(col + 1) * 128].astype(F32)
                    for k in range(STORED)
                ]
                for n, (j, k) in enumerate(PAIRS):
                    prod = v[j] * v[k]
                    accs[n] = accs[n] + prod[0:8] + prod[8:16]
            return tuple(accs)

        return lax.fori_loop(first, last, step, accs)

    accs = tuple(jnp.zeros((8, 128), F32) for _ in PAIRS)
    stages = (c2_issue, c3_issue, d1_issue, d2_issue, d3_issue, d4_issue)
    for turn in range(1, S + 7):
        for n, stage in enumerate(stages):
            if 0 <= turn - 1 - n < S:
                stage(turn - 1 - n)
        if turn + 1 < S:
            c1_issue(turn + 1)
        if turn == 1:
            for copy in ab1:
                copy.wait_recv()
            ref = ab.at[:, qy]
            ab2 = go_sent(remote(ref, ref, p_core))
        if turn <= 4:
            lax.fori_loop(6 * turn - 6, 6 * turn, tm_step, 0)
        if turn == 4:
            lax.fori_loop(0, 4, gx_step, 0)
        if 5 <= turn < 9:
            accs = gram_range(32 * turn - 160, 32 * turn - 128, accs)
        if turn == 8:
            for n in range(N_GRAM):
                stat_g[n:n + 1, :] = jnp.sum(accs[n], axis=0, keepdims=True)
            stat_g[N_GRAM:32, :] = jnp.zeros((32 - N_GRAM, 128), F32)
            gram_sum = all_sum(stat_g, slot_gy, slot_gx)
            next(gram_sum)
        if turn == 9:
            next(gram_sum)
        s = turn - 7
        if 0 <= s < S:
            for copy in d4[s]:
                copy.wait_recv()
            if s < S - 1:
                grad(s)
    ab2[0].wait_recv()

    def last_grad(half):
        def step(i, carry):
            p, n = i // 2, i % 2
            grad_step(S - 1, p * 4 + half * 2 + n)
            return carry

        lax.fori_loop(0, 4, step, 0)
        for i in range(2):
            b_q, a_q = ab[1, half * 2 + i], ab[0, half * 2 + i]
            rows = slice(i * 128, i * 128 + 128)
            pa[half, rows, :] = gacc[1, half, rows, :] * a_q + gacc[0, half, rows, :] * b_q

    last_grad(1 - c)
    e1 = go_sent(remote(pa.at[1 - c], rg, p_core))
    last_grad(c)
    own = pl.ds(pl.multiple_of(yl * 128, 128), 128)
    other = pl.ds(pl.multiple_of((1 - yl) * 128, 128), 128)
    e1[0].wait_recv()
    sy[...] = (pa[c, other, :] + rg[other, :]).astype(E_Y)
    e2 = go_sent(remote(sy, ry, p_yl))
    e2[0].wait_recv()
    adj[q] = (pa[c, own, :] + rg[own, :] + ry[...].astype(F32)).astype(BF16)
    e3 = go_sent(
        remote(adj.at[q], adj.at[q], p_yl),
        remote(adj.at[q], adj.at[q], p_core),
    )
    means = next(gram_sum)
    gram = {}
    for n, (j, k) in enumerate(PAIRS):
        gram[j, k] = gram[k, j] = means[n:n + 1, :]
    lower = {}
    inverse = []
    for j in range(STORED):
        pivot = gram[j, j]
        for n in range(j):
            pivot = pivot - lower[j, n] * lower[j, n]
        pivot = jnp.sqrt(pivot)
        inverse.append(1.0 / pivot)
        for i in range(j + 1, STORED):
            entry = gram[i, j]
            for n in range(j):
                entry = entry - lower[i, n] * lower[j, n]
            lower[i, j] = entry * inverse[j]
    e3[0].wait_recv()
    e4 = go_sent(remote(adj.at[qy], adj.at[qy], p_core))
    e3[1].wait_recv()
    e4[0].wait_recv()
    ao = pltpu.make_async_copy(adj, adj_out, lsem.at[8])
    ao.start()

    for k in range(STORED):
        total = jnp.zeros((1, 128), F32)
        for i in range(4):
            right = adj[i].astype(F32)
            if k == 6:
                for j in range(J):
                    left = part[j, 2, i // 2, (i % 2) * 2:(i % 2) * 2 + 2].reshape(128, 256)
                    total = total + fold(left * right[:, j * 256:j * 256 + 256])
            else:
                total = total + fold(tmat[k, i * 128:i * 128 + 128, :] * right)
        stat_c[k:k + 1, :] = total
    whole = adj[...].reshape(512, 512)
    total = jnp.zeros((1, 128), F32)
    for i in range(2):
        rows = slice(i * 256, i * 256 + 256)
        mixed = dot(gx[0, rows, :], whole) + dot(gx[1, rows, :], whole)
        total = total + fold(mixed * whole[i * 256:i * 256 + 256].astype(F32))
    stat_c[7:8, :] = total

    corr_sum = all_sum(stat_c, slot_cy, slot_cx)
    next(corr_sum)
    next(corr_sum)
    means = next(corr_sum)
    corr = [means[n:n + 1, :] for n in range(STORED)]
    power = means[7:8, :]
    forward = []
    for j in range(STORED):
        running = corr[j]
        for n in range(j):
            running = running - lower[j, n] * forward[n]
        forward.append(running * inverse[j])
    load = [None] * STORED
    for j in reversed(range(STORED)):
        running = forward[j]
        for n in range(j + 1, STORED):
            running = running - lower[n, j] * load[n]
        load[j] = running * inverse[j]
    rest = power
    for j in range(STORED):
        inner = -2.0 * corr[j]
        for k in range(STORED):
            inner = inner + gram[j, k] * load[k]
        rest = rest + load[j] * inner
    rest = jnp.maximum(rest, 0.0)
    scale = 1.0 / jnp.sqrt(rest + 1e-06)
    share = jnp.sqrt((rest + 1e-06) / (power + 1e-06))
    rows = [-(load[j] * scale) for j in range(STORED)] + [scale, share]
    rows = rows + [jnp.zeros((1, 1), F32)] * (16 - len(rows))
    for n in range(16):
        coef_out[n:n + 1, :] = jnp.broadcast_to(rows[n], (1, 128))

    for copy in sent:
        copy.wait_send()
    xo.wait()
    ao.wait()


def final_kernel(coef, x_ref, adj_ref, st_ref, out_ref, share_ref):
    @pl.when(pl.program_id(0) == 0)
    def _():
        share_ref[0] = coef[8, 0]

    left = x_ref[0].reshape(512, x_ref.shape[-1])
    image = lax.dot_general(
        left, adj_ref[...], (((0,), (0,)), ((), ())), preferred_element_type=F32
    )
    total = image * coef[7, 0]
    for k in range(STORED):
        total = total + coef[k, 0] * st_ref[k].astype(F32)
    out_ref[...] = total


def body(inputs, targets, gate_weight, up_weight, down_weight, stored_vectors):
    any_spec = pl.BlockSpec(memory_space=pl.ANY)
    n_copies = 220
    adj, xg, coef = pl.pallas_call(
        comm_kernel,
        out_shape=(
            jax.ShapeDtypeStruct((4, 128, 512), BF16),
            jax.ShapeDtypeStruct((2, 2, 4, 4, 16, 1024), BF16),
            jax.ShapeDtypeStruct((16, 128), F32),
        ),
        in_specs=[any_spec] * 6,
        out_specs=(any_spec, any_spec, pl.BlockSpec(memory_space=pltpu.VMEM)),
        scratch_shapes=[
            pltpu.VMEM((2, 2, 4, 4, 16, 1024), BF16),
            pltpu.VMEM((16, 2048), BF16),
            pltpu.VMEM((2048, 512), BF16),
            pltpu.VMEM((2048, 512), BF16),
            pltpu.VMEM((512, 2048), BF16),
            pltpu.VMEM((STORED, 2048, 512), BF16),
            pltpu.VMEM((J, 3, 2, 4, 4, 16, 256), F32),
            pltpu.VMEM((J, 3, 4, 4, 16, 256), F32),
            pltpu.VMEM((J, 3, 2, 4, 16, 256), B_Y),
            pltpu.VMEM((J, 3, 2, 4, 16, 256), B_Y),
            pltpu.VMEM((STORED - 1, 512, 512), F32),
            pltpu.VMEM((2, 512, 512), BF16),
            pltpu.VMEM((J, 2, 4, 128, 256), BF16),
            pltpu.VMEM((2, 4, 128, 512), F32),
            pltpu.VMEM((S, 2, 4, 4, 4, 16, W), C1),
            pltpu.VMEM((S, 2, 3, 4, 4, 16, W), C1),
            pltpu.VMEM((S, 2, 2, 4, 16, W), C2),
            pltpu.VMEM((S, 2, 2, 4, 16, W), F32),
            pltpu.VMEM((S, 2, 2, 4, 16, W), C2),
            pltpu.VMEM((S, 2, 2, 4, 16, W), C3),
            pltpu.VMEM((S, 2, 2, 4, 16, W), F32),
            pltpu.VMEM((S, 2, 3, 2, 16, W), C3),
            pltpu.VMEM((S, 2, 2, 2, 4, 4, 16, W), BF16),
            pltpu.VMEM((2, 2, 256, 512), F32),
            pltpu.VMEM((2, 256, 512), F32),
            pltpu.VMEM((256, 512), F32),
            pltpu.VMEM((128, 512), E_Y),
            pltpu.VMEM((128, 512), E_Y),
            pltpu.VMEM((4, 128, 512), BF16),
            pltpu.VMEM((32, 128), F32),
            pltpu.VMEM((8, 32, 128), F32),
            pltpu.VMEM((16, 32, 128), F32),
            pltpu.VMEM((8, 128), F32),
            pltpu.VMEM((8, 8, 128), F32),
            pltpu.VMEM((16, 8, 128), F32),
            pltpu.SemaphoreType.DMA((9,)),
            pltpu.SemaphoreType.DMA((n_copies,)),
            pltpu.SemaphoreType.DMA((n_copies,)),
        ],
        compiler_params=pltpu.CompilerParams(
            collective_id=0, has_side_effects=True, vmem_limit_bytes=62 * 2**20
        ),
        name="exchange",
    )(inputs, targets, gate_weight, up_weight, down_weight, stored_vectors)

    tile = 256
    per_half = 1024 // tile
    next_vector, share = pl.pallas_call(
        final_kernel,
        grid=(2048 // tile,),
        out_shape=(
            jax.ShapeDtypeStruct((2048, 512), F32),
            jax.ShapeDtypeStruct((1,), F32),
        ),
        in_specs=[
            pl.BlockSpec(memory_space=pltpu.SMEM),
            pl.BlockSpec((1, 512, tile), lambda i: (i // per_half, 0, i % per_half)),
            pl.BlockSpec((512, 512), lambda i: (0, 0)),
            pl.BlockSpec((STORED, tile, 512), lambda i: (0, i, 0)),
        ],
        out_specs=(
            pl.BlockSpec((tile, 512), lambda i: (i, 0)),
            pl.BlockSpec(memory_space=pltpu.SMEM),
        ),
        compiler_params=pltpu.CompilerParams(vmem_limit_bytes=60 * 2**20),
        name="finish",
    )(coef, xg.reshape(2, 512, 1024), adj.reshape(512, 512), stored_vectors)
    return next_vector, share


def solution(mesh):
    return jax.shard_map(
        body,
        mesh=mesh,
        in_specs=(
            P("ffn", "mp"),
            P("ffn", "mp"),
            P("mp", "ffn"),
            P("mp", "ffn"),
            P("ffn", "mp"),
            P(None, "mp", "ffn"),
        ),
        out_specs=(P("mp", "ffn"), P()),
        check_vma=False,
    )
```

time: 208 us -> 149 us (0.72)
  Pallas kernels: 199 us -> 148 us
  local copies, waits for them, and re-layouts: 8.5 us -> 0 us
    pallas_call x1, Pallas kernels: 188 us -> 136 us  [body(): pl.pallas_call(comm_kernel, out_shape=(jax.ShapeDtypeStruct((4, 128, 512)...]
    unnamed x8 -> x0, local copies, waits for them, and re-layouts: 8.5 us -> none
where the time goes in v2:
time: 149 us; the launch traced here: 148 us
  Pallas kernels  148 us (99%)
    pallas_call x1, Pallas kernels, body(): pl.pallas_call(comm_kernel, out_shape=(jax.ShapeDtypeStruct((4, 128, 512)...  136 us
    pallas_call x1, Pallas kernels, body(): pl.pallas_call(final_kernel, grid=(2048 // tile,), out_shape=(jax.ShapeDt...  11.5 us

profile of v2, /device:TPU:0, one launch (start us, length us, event | category | flops | bytes accessed | tf_op | source)
XLA Modules:
  0.0 148.3 jit_solution(9592869563821010482)
XLA Ops:
  0.6 136.1 %exchange.1 = (bf16[4,128,512]{2,1,0:T(8,128)(2,1)}, bf16[2,2,4,4,16,1024]{5,4,3,2,1,0:T(8,128)(2,1)}, f32[16,128]{1,0:T(8,128)}) custom-call(bf16[16,2048]{1,0:T(8,128)(2,1)} %x_hbm.1, bf16[16,2048]{1,0:T(8,128)(2,1)} %tgt_hbm.1, bf16[2048,512]{1,0:T(8,128)(2,1)} %gate_hbm.1, bf16[2048,512]{1,0:T(8,128)(2,1)} %up_hbm.1, bf16[512,2048]{1,0:T(8,128)(2,1)} %down_hbm.1, ...), custom_call_target="tpu_custom_call" | custom-call | tf_op jit(solution)/shard_map/exchange/pallas_call | solution.py:573
  136.8 11.5 %finish.1 = (f32[2048,512]{1,0:T(8,128)}, f32[1]{0:T(128)}) custom-call(f32[16,128]{1,0:T(8,128)} %get-tuple-element.5.coef, bf16[2,512,1024]{2,1,0:T(8,128)(2,1)} %bitcast.2, bf16[512,512]{1,0:T(8,128)(2,1)} %bitcast.3, bf16[7,2048,512]{2,1,0:T(8,128)(2,1)} %st_ref.1), custom_call_target="tpu_custom_call" | custom-call | tf_op jit(solution)/shard_map/finish/pallas_call | solution.py:630

commit v3 on v2

--- a/solution.py
+++ b/solution.py
@@ -22,8 +22,7 @@
 C3 = BF16
 E_Y = BF16
 S = 4
-W = 1024 // S
-J = 2
+W = 256
 
 
 def dot(left, right):
@@ -75,7 +74,7 @@
         at(x_=(x + i) % 4, z_=(z + j) % 4) for i in range(4) for j in range(4) if i + j > 0
     ]
     p_core, p_yl, p_yh = at(c_=1 - c), at(yl_=1 - yl), at(yh_=1 - yh)
-    peers = p_yc + p_xz
+    peers = [p_core, p_yl, p_yh] + p_x + p_z
 
     counter = [0]
 
@@ -107,7 +106,7 @@
         pltpu.make_async_copy(up_hbm, up_w, lsem.at[3]),
         pltpu.make_async_copy(stored_hbm, st, lsem.at[4]),
         pltpu.make_async_copy(down_hbm, down_w, lsem.at[5]),
-        pltpu.make_async_copy(tgt_hbm, tgt, lsem.at[6]),
+        pltpu.make_async_copy(tgt_hbm, tgt.at[yh], lsem.at[6]),
     ]
     go(*loads)
     go(*late)
@@ -115,9 +114,9 @@
     barrier = pltpu.get_barrier_semaphore()
     for who in peers:
         pl.semaphore_signal(barrier, inc=1, device_id=who, device_id_type=MESH)
-    for j in range(J):
+    for t in range(2):
         for n in range(3):
-            part[j, n] = jnp.zeros(part.shape[2:], F32)
+            part[t, n] = jnp.zeros(part.shape[2:], F32)
     pl.semaphore_wait(barrier, len(peers))
     for copy in loads:
         copy.wait()
@@ -137,112 +136,111 @@
                 remote(block(1, w), block(1, w), p_x[d]),
             )
 
-    def third(i, w):
+    def third(t):
+        a3[t] = []
+        for d in range(3):
+            a3[t] += go_sent(
+                remote(xg.at[0, t, x], xg.at[0, t, x], p_x[d]),
+                remote(xg.at[1, t, :, z], xg.at[1, t, :, z], p_z[d]),
+            )
+
+    second(0, yh)
+    a1[0].wait_recv()
+    second(1, 1 - yh)
+    for i in range(2):
         for copy in a2[i]:
             copy.wait_recv()
-        a3[i] = []
-        for d in range(3):
-            a3[i] += go_sent(
-                remote(xg.at[0, w, x], xg.at[0, w, x], p_x[d]),
-                remote(xg.at[1, w, :, z], xg.at[1, w, :, z], p_z[d]),
-            )
-
-    mine, far = yh, 1 - yh
-    second(0, mine)
-    a1[0].wait_recv()
-    second(1, far)
-    third(0, mine)
-    third(1, far)
+    third(0)
+    third(1)
     for copy in late:
         copy.wait()
-
-    def partial(h, line):
+    goal = go_sent(remote(tgt.at[yh], tgt.at[yh], p_yh))
+
+    def partial(t, h, lines):
         def step(j, carry):
             cols = pl.ds(pl.multiple_of(j * 256, 256), 256)
-            left = (xg[0, :, line] if h == 0 else xg[1, :, :, line]).reshape(128, 1024)
+            left = jnp.concatenate(
+                [(xg[0, t, l] if h == 0 else xg[1, t, :, l]).reshape(64, 1024) for l in lines], axis=0
+            )
             depth = slice(h * 1024, h * 1024 + 1024)
             for n in range(3):
                 right = (gate_w, up_w)[n][depth, cols] if n < 2 else st[6, depth, cols]
-                value = dot(left, right).reshape(2, 4, 16, 256)
-                if h == 0:
-                    part[j, n, :, line] = part[j, n, :, line] + value
-                else:
-                    part[j, n, :, :, line] = part[j, n, :, :, line] + value
+                value = dot(left, right)
+                for i, l in enumerate(lines):
+                    piece = value[i * 64:i * 64 + 64].reshape(4, 16, 256)
+                    if h == 0:
+                        part[t, n, l, :, :, cols] = part[t, n, l, :, :, cols] + piece
+                    else:
+                        part[t, n, :, l, :, cols] = part[t, n, :, l, :, cols] + piece
             return carry
 
-        lax.fori_loop(0, J, step, 0)
-
-    partial(0, x)
-    partial(1, z)
-    for d, source in ((0, 1), (1, 0), (2, 2)):
-        a3[0][2 * d].wait_recv()
-        a3[1][2 * d].wait_recv()
-        partial(0, xs[source])
-        a3[0][2 * d + 1].wait_recv()
-        a3[1][2 * d + 1].wait_recv()
-        partial(1, zs[source])
-
-    b1 = []
-    for j in range(J):
-        b1 += go_sent(remote(part.at[j, :, 1 - c], rb.at[j], p_core))
-    b2 = []
-    for j in range(J):
-        b1[j].wait_recv()
+        lax.fori_loop(0, 2, step, 0)
+
+    def partials(t):
+        a3[t][0].wait_recv()
+        partial(t, 0, (x, xs[1]))
+        a3[t][1].wait_recv()
+        partial(t, 1, (z, zs[1]))
+        a3[t][2].wait_recv()
+        a3[t][4].wait_recv()
+        partial(t, 0, (xs[0], xs[2]))
+        a3[t][3].wait_recv()
+        a3[t][5].wait_recv()
+        partial(t, 1, (zs[0], zs[2]))
+
+    b1, b2, b3, b4 = {}, {}, {}, {}
+
+    def b_core(t):
+        b1[t] = go_sent(remote(part.at[t, :, pl.ds((1 - c) * 2, 2)], rb.at[t], p_core))
+
+    def b_y(t):
+        b1[t][0].wait_recv()
         for n in range(3):
-            for i in range(2):
-                g = (1 - yl) * 2 + i
-                sby[j, n, i] = (part[j, n, c, g] + rb[j, n, g]).astype(B_Y)
-        b2 += go_sent(remote(sby.at[j], rby.at[j], p_yl))
-    b3 = []
-    for j in range(J):
-        cols = slice(j * 256, j * 256 + 256)
-        sums = []
-        b2[j].wait_recv()
-        for n in range(3):
-            halves = []
-            for i in range(2):
-                g = yl * 2 + i
-                halves.append(part[j, n, c, g] + rb[j, n, g] + rby[j, n, i].astype(F32))
-            sums.append(jnp.concatenate([v.reshape(64, 256) for v in halves], axis=0))
-        gate, upv, tang = sums
+            sby[t, n] = (part[t, n, qy] + rb[t, n, 1 - yl]).astype(B_Y)
+        b2[t] = go_sent(remote(sby.at[t], rby.at[t], p_yl))
+
+    def b_hidden(t):
+        b2[t][0].wait_recv()
+        gate, upv, tang = [
+            (part[t, n, q] + rb[t, n, yl] + rby[t, n].astype(F32)).reshape(64, 512)
+            for n in range(3)
+        ]
         sg = 1.0 / (1.0 + jnp.exp(-gate))
         swish = gate * sg
         slope = sg * (1.0 + gate * (1.0 - sg))
         curve = sg * (1.0 - sg) * (2.0 + gate * (1.0 - 2.0 * sg))
-        hp[j, 0, q] = (swish * upv).astype(BF16)
-        hp[j, 1, q] = (slope * upv * tang).astype(BF16)
-        ref = hp.at[j, :, q]
-        b3.append(go_sent(remote(ref, ref, p_yl), remote(ref, ref, p_core)))
-        ab[0, q, :, cols] = upv * slope
-        ab[1, q, :, cols] = upv * curve * tang
-    b4 = []
-    for j in range(J):
-        b3[j][0].wait_recv()
-        ref = hp.at[j, :, qy]
-        b4 += go_sent(remote(ref, ref, p_core))
-    for j in range(J):
-        b3[j][1].wait_recv()
-        b4[j].wait_recv()
-
-    own_ab = ab.at[:, q]
-    ab1 = go_sent(remote(own_ab, own_ab, p_yl), remote(own_ab, own_ab, p_core))
+        hp[t, 0, q] = (swish * upv).astype(BF16)
+        hp[t, 1, q] = (slope * upv * tang).astype(BF16)
+        ref = hp.at[t, :, q]
+        b3[t] = go_sent(remote(ref, ref, p_yl), remote(ref, ref, p_core))
+        ab[t, 0, q] = upv * slope
+        ab[t, 1, q] = upv * curve * tang
+
+    def b_forward(t):
+        b3[t][0].wait_recv()
+        ref = hp.at[t, :, qy]
+        b4[t] = go_sent(remote(ref, ref, p_core))
+
+    def b_done(t):
+        b3[t][1].wait_recv()
+        b4[t][0].wait_recv()
+
     c1, c2, c3, d1, d2, d3, d4 = {}, {}, {}, {}, {}, {}, {}
+
+    def first_col(s, h, u):
+        return h * 1024 + u * 512 + (s % 2) * W
 
     def c1_issue(s):
         c1[s] = []
-        for h in range(2):
-            def out_step(r, carry, h=h):
-                wide = slice(h * 1024 + s * W, h * 1024 + s * W + W)
-                value = jnp.zeros((256, W), F32)
-                for j in range(J):
-                    left = hp[j, r // 2, pl.ds((r % 2) * 2, 2)].reshape(256, 256)
-                    value = value + dot(left, down_w[j * 256:j * 256 + 256, wide])
-                s1[s, h, r] = value.astype(C1).reshape(4, 4, 16, W)
-                return carry
-
-            lax.fori_loop(0, 4, out_step, 0)
+        t = s // 2
+        for u in range(2):
+            for r in range(4):
+                p, h = r // 2, r % 2
+                col = first_col(s, h, u)
+                value = dot(hp[t, p].reshape(256, 512), down_w[:, col:col + W])
+                s1[s, u, r] = value.astype(C1).reshape(4, 4, 16, W)
             for d in range(3):
-                if h == 0:
+                if u == 0:
                     c1[s] += go_sent(remote(s1.at[s, 0, :, :, zs[d]], r1.at[s, 0, d], p_z[d]))
                 else:
                     c1[s] += go_sent(remote(s1.at[s, 1, :, xs[d]], r1.at[s, 1, d], p_x[d]))
@@ -294,8 +292,8 @@
                 for d in range(3):
                     total = total + r3[s, h, d, p].astype(F32)
                 if p == 0:
-                    wide = slice(h * 1024 + s * W, h * 1024 + s * W + W)
-                    total = total - tgt[:, wide].astype(F32)
+                    wide = pl.ds(pl.multiple_of(first_col(s, yh, h), W), W)
+                    total = total - tgt[s // 2, :, wide].astype(F32)
                 rp[s, h, p, yh, x, z] = total.astype(BF16)
             ref = rp.at[s, h, :, yh, x, z]
             for d in range(3):
@@ -325,8 +323,25 @@
             ref = rp.at[s, 1, d, :, xs[1 - d]]
             d4[s] += go_sent(remote(ref, ref, p_x[d]))
 
+    partials(0)
+    b_core(0)
+    b_y(0)
+    partials(1)
+    b_core(1)
+    b_hidden(0)
+    b_y(1)
+    b_forward(0)
+    b_done(0)
     c1_issue(0)
     c1_issue(1)
+    b_hidden(1)
+    b_forward(1)
+    ab1 = []
+    for t in range(2):
+        ref = ab.at[t, :, q]
+        ab1 += go_sent(remote(ref, ref, p_yl), remote(ref, ref, p_core))
+    b_done(1)
+    goal[0].wait_recv()
 
     def x_rows(h, half):
         return xg[h, half].reshape(256, 1024)
@@ -353,23 +368,61 @@
     xo = pltpu.make_async_copy(xg, x_out, lsem.at[7])
     xo.start()
 
-    def grad_step(s, i):
-        p, half, n = i // 4, (i // 2) % 2, i % 2
-        rows = pl.ds(pl.multiple_of(n * 256, 256), 256)
-        value = dot_nt(rp[s, 0, p, half].reshape(256, W), down_w[rows, s * W:s * W + W])
-        value = value + dot_nt(
-            rp[s, 1, p, half].reshape(256, W), down_w[rows, 1024 + s * W:1024 + s * W + W]
-        )
-        if s > 0:
-            value = value + gacc[p, half, :, rows]
-        gacc[p, half, :, rows] = value
-
     def grad(s):
-        def step(i, carry):
-            grad_step(s, i)
-            return carry
-
-        lax.fori_loop(0, 8, step, 0)
+        t = s // 2
+        for p in range(2):
+            def step(n, carry, p=p):
+                rows = pl.ds(pl.multiple_of(n * 256, 256), 256)
+                value = jnp.zeros((256, 256), F32)
+                for u in range(2):
+                    for h in range(2):
+                        col = first_col(s, h, u)
+                        value = value + dot_nt(rp[s, u, p, h].reshape(256, W), down_w[rows, col:col + W])
+                if s % 2:
+                    value = value + gacc[t, p, :, rows]
+                gacc[t, p, :, rows] = value
+                return carry
+
+            lax.fori_loop(0, 2, step, 0)
+
+    e1, e2, e3, e4 = {}, {}, {}, {}
+
+    def e_core(t):
+        for i in range(4):
+            rows = slice(i * 64, i * 64 + 64)
+            pa[t, i] = gacc[t, 1, rows, :] * ab[t, 0, i] + gacc[t, 0, rows, :] * ab[t, 1, i]
+        e1[t] = go_sent(remote(pa.at[t, pl.ds((1 - c) * 2, 2)], rg.at[t], p_core))
+
+    def e_y(t):
+        e1[t][0].wait_recv()
+        sy[t] = (pa[t, qy] + rg[t, 1 - yl]).astype(E_Y)
+        e2[t] = go_sent(remote(sy.at[t], ry.at[t], p_yl))
+
+    def e_adjoint(t):
+        e2[t][0].wait_recv()
+        adj[t, q] = (pa[t, q] + rg[t, yl] + ry[t].astype(F32)).astype(BF16)
+        ref = adj.at[t, q]
+        e3[t] = go_sent(remote(ref, ref, p_yl), remote(ref, ref, p_core))
+
+    def e_forward(t):
+        e3[t][0].wait_recv()
+        e4[t] = go_sent(remote(adj.at[t, qy], adj.at[t, qy], p_core))
+
+    def e_done(t):
+        e3[t][1].wait_recv()
+        e4[t][0].wait_recv()
+
+    def correlate(t):
+        for k in range(STORED):
+            total = jnp.zeros((1, 128), F32) if t == 0 else stat_c[k:k + 1, :]
+            for i in range(2):
+                right = adj[t, 2 * i:2 * i + 2].reshape(128, 512).astype(F32)
+                if k == 6:
+                    left = part[t, 2, 2 * i:2 * i + 2].reshape(128, 512)
+                else:
+                    left = tmat[k, t * 256 + i * 128:t * 256 + i * 128 + 128, :]
+                total = total + fold(left * right)
+            stat_c[k:k + 1, :] = total
 
     def all_sum(stat, slot_y, slot_x):
         mine = (yh * 2 + yl) * 2 + c
@@ -421,7 +474,7 @@
         if turn == 1:
             for copy in ab1:
                 copy.wait_recv()
-            ref = ab.at[:, qy]
+            ref = ab.at[:, :, qy]
             ab2 = go_sent(remote(ref, ref, p_core))
         if turn <= 4:
             lax.fori_loop(6 * turn - 6, 6 * turn, tm_step, 0)
@@ -437,40 +490,24 @@
             next(gram_sum)
         if turn == 9:
             next(gram_sum)
+        if turn == 9:
+            e_y(0)
+        if turn == 10:
+            e_adjoint(0)
         s = turn - 7
         if 0 <= s < S:
             for copy in d4[s]:
                 copy.wait_recv()
-            if s < S - 1:
-                grad(s)
-    ab2[0].wait_recv()
-
-    def last_grad(half):
-        def step(i, carry):
-            p, n = i // 2, i % 2
-            grad_step(S - 1, p * 4 + half * 2 + n)
-            return carry
-
-        lax.fori_loop(0, 4, step, 0)
-        for i in range(2):
-            b_q, a_q = ab[1, half * 2 + i], ab[0, half * 2 + i]
-            rows = slice(i * 128, i * 128 + 128)
-            pa[half, rows, :] = gacc[1, half, rows, :] * a_q + gacc[0, half, rows, :] * b_q
-
-    last_grad(1 - c)
-    e1 = go_sent(remote(pa.at[1 - c], rg, p_core))
-    last_grad(c)
-    own = pl.ds(pl.multiple_of(yl * 128, 128), 128)
-    other = pl.ds(pl.multiple_of((1 - yl) * 128, 128), 128)
-    e1[0].wait_recv()
-    sy[...] = (pa[c, other, :] + rg[other, :]).astype(E_Y)
-    e2 = go_sent(remote(sy, ry, p_yl))
-    e2[0].wait_recv()
-    adj[q] = (pa[c, own, :] + rg[own, :] + ry[...].astype(F32)).astype(BF16)
-    e3 = go_sent(
-        remote(adj.at[q], adj.at[q], p_yl),
-        remote(adj.at[q], adj.at[q], p_core),
-    )
+            grad(s)
+            if s == 0:
+                ab2[0].wait_recv()
+            if s % 2:
+                e_core(s // 2)
+    e_forward(0)
+    e_y(1)
+    e_done(0)
+    correlate(0)
+    e_adjoint(1)
     means = next(gram_sum)
     gram = {}
     for n, (j, k) in enumerate(PAIRS):
@@ -488,24 +525,12 @@
             for n in range(j):
                 entry = entry - lower[i, n] * lower[j, n]
             lower[i, j] = entry * inverse[j]
-    e3[0].wait_recv()
-    e4 = go_sent(remote(adj.at[qy], adj.at[qy], p_core))
-    e3[1].wait_recv()
-    e4[0].wait_recv()
+    e_forward(1)
+    e_done(1)
     ao = pltpu.make_async_copy(adj, adj_out, lsem.at[8])
     ao.start()
 
-    for k in range(STORED):
-        total = jnp.zeros((1, 128), F32)
-        for i in range(4):
-            right = adj[i].astype(F32)
-            if k == 6:
-                for j in range(J):
-                    left = part[j, 2, i // 2, (i % 2) * 2:(i % 2) * 2 + 2].reshape(128, 256)
-                    total = total + fold(left * right[:, j * 256:j * 256 + 256])
-            else:
-                total = total + fold(tmat[k, i * 128:i * 128 + 128, :] * right)
-        stat_c[k:k + 1, :] = total
+    correlate(1)
     whole = adj[...].reshape(512, 512)
     total = jnp.zeros((1, 128), F32)
     for i in range(2):
@@ -573,7 +598,7 @@
     adj, xg, coef = pl.pallas_call(
         comm_kernel,
         out_shape=(
-            jax.ShapeDtypeStruct((4, 128, 512), BF16),
+            jax.ShapeDtypeStruct((2, 4, 64, 512), BF16),
             jax.ShapeDtypeStruct((2, 2, 4, 4, 16, 1024), BF16),
             jax.ShapeDtypeStruct((16, 128), F32),
         ),
@@ -581,19 +606,19 @@
         out_specs=(any_spec, any_spec, pl.BlockSpec(memory_space=pltpu.VMEM)),
         scratch_shapes=[
             pltpu.VMEM((2, 2, 4, 4, 16, 1024), BF16),
-            pltpu.VMEM((16, 2048), BF16),
+            pltpu.VMEM((2, 16, 2048), BF16),
             pltpu.VMEM((2048, 512), BF16),
             pltpu.VMEM((2048, 512), BF16),
             pltpu.VMEM((512, 2048), BF16),
             pltpu.VMEM((STORED, 2048, 512), BF16),
-            pltpu.VMEM((J, 3, 2, 4, 4, 16, 256), F32),
-            pltpu.VMEM((J, 3, 4, 4, 16, 256), F32),
-            pltpu.VMEM((J, 3, 2, 4, 16, 256), B_Y),
-            pltpu.VMEM((J, 3, 2, 4, 16, 256), B_Y),
+            pltpu.VMEM((2, 3, 4, 4, 16, 512), F32),
+            pltpu.VMEM((2, 3, 2, 4, 16, 512), F32),
+            pltpu.VMEM((2, 3, 4, 16, 512), B_Y),
+            pltpu.VMEM((2, 3, 4, 16, 512), B_Y),
             pltpu.VMEM((STORED - 1, 512, 512), F32),
             pltpu.VMEM((2, 512, 512), BF16),
-            pltpu.VMEM((J, 2, 4, 128, 256), BF16),
-            pltpu.VMEM((2, 4, 128, 512), F32),
+            pltpu.VMEM((2, 2, 4, 64, 512), BF16),
+            pltpu.VMEM((2, 2, 4, 64, 512), F32),
             pltpu.VMEM((S, 2, 4, 4, 4, 16, W), C1),
             pltpu.VMEM((S, 2, 3, 4, 4, 16, W), C1),
             pltpu.VMEM((S, 2, 2, 4, 16, W), C2),
@@ -604,11 +629,11 @@
             pltpu.VMEM((S, 2, 3, 2, 16, W), C3),
             pltpu.VMEM((S, 2, 2, 2, 4, 4, 16, W), BF16),
             pltpu.VMEM((2, 2, 256, 512), F32),
-            pltpu.VMEM((2, 256, 512), F32),
-            pltpu.VMEM((256, 512), F32),
-            pltpu.VMEM((128, 512), E_Y),
-            pltpu.VMEM((128, 512), E_Y),
-            pltpu.VMEM((4, 128, 512), BF16),
+            pltpu.VMEM((2, 4, 64, 512), F32),
+            pltpu.VMEM((2, 2, 64, 512), F32),
+            pltpu.VMEM((2, 64, 512), E_Y),
+            pltpu.VMEM((2, 64, 512), E_Y),
+            pltpu.VMEM((2, 4, 64, 512), BF16),
             pltpu.VMEM((32, 128), F32),
             pltpu.VMEM((8, 32, 128), F32),
             pltpu.VMEM((16, 32, 128), F32),
@@ -625,7 +650,7 @@
         name="exchange",
     )(inputs, targets, gate_weight, up_weight, down_weight, stored_vectors)
 
-    tile = 256
+    tile = 512
     per_half = 1024 // tile
     next_vector, share = pl.pallas_call(
         final_kernel,

time: 149 us -> 139 us (0.933)
  Pallas kernels: 148 us -> 139 us
    pallas_call x1, Pallas kernels: 136 us -> 129 us  [body(): pl.pallas_call(comm_kernel, out_shape=(jax.ShapeDtypeStruct((2, 4, 64, 51...]
    pallas_call x1, Pallas kernels: 11.5 us -> 9.67 us  [body(): pl.pallas_call(final_kernel, grid=(2048 // tile,), out_shape=(jax.ShapeDt...]
where the time goes in v3:
time: 139 us
  Pallas kernels  139 us (100%)
    pallas_call x1, Pallas kernels, body(): pl.pallas_call(comm_kernel, out_shape=(jax.ShapeDtypeStruct((2, 4, 64, 51...  129 us
    pallas_call x1, Pallas kernels, body(): pl.pallas_call(final_kernel, grid=(2048 // tile,), out_shape=(jax.ShapeDt...  9.67 us

profile of v3, /device:TPU:0, one launch (start us, length us, event | category | flops | bytes accessed | tf_op | source)
XLA Modules:
  0.0 139.3 jit_solution(2363803373406083175)
XLA Ops:
  0.6 129.0 %exchange.1 = (bf16[2,4,64,512]{3,2,1,0:T(8,128)(2,1)}, bf16[2,2,4,4,16,1024]{5,4,3,2,1,0:T(8,128)(2,1)}, f32[16,128]{1,0:T(8,128)}) custom-call(bf16[16,2048]{1,0:T(8,128)(2,1)} %x_hbm.1, bf16[16,2048]{1,0:T(8,128)(2,1)} %tgt_hbm.1, bf16[2048,512]{1,0:T(8,128)(2,1)} %gate_hbm.1, bf16[2048,512]{1,0:T(8,128)(2,1)} %up_hbm.1, bf16[512,2048]{1,0:T(8,128)(2,1)} %down_hbm.1, ...), custom_call_target="tpu_custom_call" | custom-call | tf_op jit(solution)/shard_map/exchange/pallas_call | solution.py:598
  129.6 9.7 %finish.1 = (f32[2048,512]{1,0:T(8,128)}, f32[1]{0:T(128)}) custom-call(f32[16,128]{1,0:T(8,128)} %get-tuple-element.5.coef, bf16[2,512,1024]{2,1,0:T(8,128)(2,1)} %bitcast.2, bf16[512,512]{1,0:T(8,128)(2,1)} %bitcast.3, bf16[7,2048,512]{2,1,0:T(8,128)(2,1)} %st_ref.1), custom_call_target="tpu_custom_call" | custom-call | tf_op jit(solution)/shard_map/finish/pallas_call | solution.py:655

commit v4 on v3

--- a/solution.py
+++ b/solution.py
@@ -650,7 +650,7 @@
         name="exchange",
     )(inputs, targets, gate_weight, up_weight, down_weight, stored_vectors)
 
-    tile = 512
+    tile = 1024
     per_half = 1024 // tile
     next_vector, share = pl.pallas_call(
         final_kernel,

time: 139 us -> 139 us (level)
  no operation moved by 1% of the time
where the time goes in v4:
time: 139 us
  Pallas kernels  138 us (99%)
    pallas_call x1, Pallas kernels, body(): pl.pallas_call(comm_kernel, out_shape=(jax.ShapeDtypeStruct((2, 4, 64, 51...  129 us
    pallas_call x1, Pallas kernels, body(): pl.pallas_call(final_kernel, grid=(2048 // tile,), out_shape=(jax.ShapeDt...  9.22 us

profile of v4, /device:TPU:0, one launch (start us, length us, event | category | flops | bytes accessed | tf_op | source)
XLA Modules:
  0.0 138.8 jit_solution(6731502532395531149)
XLA Ops:
  0.6 129.0 %exchange.1 = (bf16[2,4,64,512]{3,2,1,0:T(8,128)(2,1)}, bf16[2,2,4,4,16,1024]{5,4,3,2,1,0:T(8,128)(2,1)}, f32[16,128]{1,0:T(8,128)}) custom-call(bf16[16,2048]{1,0:T(8,128)(2,1)} %x_hbm.1, bf16[16,2048]{1,0:T(8,128)(2,1)} %tgt_hbm.1, bf16[2048,512]{1,0:T(8,128)(2,1)} %gate_hbm.1, bf16[2048,512]{1,0:T(8,128)(2,1)} %up_hbm.1, bf16[512,2048]{1,0:T(8,128)(2,1)} %down_hbm.1, ...), custom_call_target="tpu_custom_call" | custom-call | tf_op jit(solution)/shard_map/exchange/pallas_call | solution.py:598
  129.6 9.2 %finish.1 = (f32[2048,512]{1,0:T(8,128)}, f32[1]{0:T(128)}) custom-call(f32[16,128]{1,0:T(8,128)} %get-tuple-element.5.coef, bf16[2,512,1024]{2,1,0:T(8,128)(2,1)} %bitcast.2, bf16[512,512]{1,0:T(8,128)(2,1)} %bitcast.3, bf16[7,2048,512]{2,1,0:T(8,128)(2,1)} %st_ref.1), custom_call_target="tpu_custom_call" | custom-call | tf_op jit(solution)/shard_map/finish/pallas_call | solution.py:655
